TPU v7x, 512 devices: a whole 4x4x16 slice. The times are simulated.
512 devices in a mesh: rep: 32 (over z_lo, y), tp: 16 (over x, z_hi, core).
Axes of the slice: x: 4, y: 4, z: 16 (z_hi: 2, z_lo: 8; z = z_hi * 8 + z_lo), core: 2. Of those that a mesh axis runs over, the one named last changes fastest.
Arguments:
- queries: bfloat16 [4, 512, 8192], P(None, 'rep', 'tp'), may hold values from -240 to 240
- new_kv: bfloat16 [4, 512, 2048], P(None, 'rep', 'tp'), may hold values from -6 to 6
- kv_pool: bfloat16 [2048, 16, 16, 256], P('rep', 'tp'), may hold values from -6 to 6
- page_table: int32 [512, 8], P('rep'), may hold values from 0 to 63, as said below
- kv_lengths: int32 [512], replicated, may hold values from 1 to 128
- slot_source: int32 [512], replicated, may hold values from 0 to 511, as said below
- mamba_x: bfloat16 [4, 512, 16384], P(None, 'rep', 'tp'), may hold values from -6 to 6
- mamba_z: bfloat16 [4, 512, 16384], P(None, 'rep', 'tp'), may hold values from -6 to 6
- conv_state: bfloat16 [512, 3, 16384], P('rep', None, 'tp'), may hold values from -6 to 6
- ssm_state: float32 [512, 16, 16384], P('rep', None, 'tp'), may hold values from -6 to 6
- x_proj_weight: bfloat16 [544, 16384], P(None, 'tp'), may hold values from -0.046875 to 0.046875
- dt_proj_weight: bfloat16 [512, 16384], P(None, 'tp'), may hold values from -0.25 to 0.25
- dt_bias: float32 [16384], P('tp'), may hold values from -3 to 0.5
- a_rate: float32 [16, 16384], P(None, 'tp'), may hold values from 0.02 to 8
- skip_gain: float32 [16384], P('tp'), may hold values from 0.5 to 2
- conv_weight: float32 [4, 16384], P(None, 'tp'), may hold values from -3 to 3
- conv_bias: float32 [16384], P('tp'), may hold values from -3 to 3
- dt_gain: float32 [512], replicated, may hold values from 0.25 to 1.75
- b_gain: float32 [16], replicated, may hold values from 0.25 to 1.75
- c_gain: float32 [16], replicated, may hold values from 0.25 to 1.75
Outputs:
- attention_out: bfloat16 [4, 512, 8192], P(None, 'rep', 'tp')
- mixer_out: bfloat16 [4, 512, 16384], P(None, 'rep', 'tp')
Inputs may be any that keep to these rules, and one draw needn't show every extreme that they name: `slot_source`: A permutation of the slots. In each group exactly 2 slots take a request from another group, from 2 different groups, and each group gives exactly 2 requests away; every other slot keeps its own request. `page_table`: within a group, the pool pages of all its requests' even pages are distinct, and so are those of the odd pages.
All inputs are finite; a program needn't handle non-finite values.
Results may differ from a plain program's by a relative error of at most 0.008.
Values may be sent and summed in bfloat16 or wider, within the bound.
A program may use at most 64 MiB of HBM per device.

v0:
```python
import math

import jax
import jax.numpy as jnp
from jax import lax
from jax.sharding import PartitionSpec as P

MOVE = 2


epsilon = 1e-06
masked_score = -1e30


def swapped(value, axis, distance):
    return lax.ppermute(value, axis, [(i, i ^ 1 << distance) for i in range(lax.axis_size(axis))])


def rms_scale(values, gain):
    return values * lax.rsqrt(jnp.mean(values * values, axis=-1, keepdims=True) + epsilon) * gain


def mixer_steps(x_steps, z_steps, conv_rows, scan_state, weights):
    (
        x_proj_weight,
        dt_proj_weight,
        dt_bias,
        a_rate,
        skip_gain,
        conv_weight,
        conv_bias,
        dt_gain,
        b_gain,
        c_gain,
    ) = weights
    dt_rank = dt_proj_weight.shape[0]
    state_size = a_rate.shape[0]
    activations = []
    for step_idx in range(x_steps.shape[0]):
        window = jnp.concatenate([conv_rows, x_steps[step_idx][:, None, :]], axis=1)
        activations.append(
            jax.nn.silu(jnp.sum(window.astype(jnp.float32) * conv_weight[None], axis=1) + conv_bias)
        )
        conv_rows = window[:, 1:, :]
    activ = jnp.stack(activations)
    partial_terms = jnp.einsum(
        "src,kc->srk", activ.astype(jnp.bfloat16), x_proj_weight, preferred_element_type=jnp.float32
    )
    projected = lax.psum(partial_terms, "tp")
    outputs = []
    for step_idx in range(x_steps.shape[0]):
        dt_low = rms_scale(projected[step_idx, :, :dt_rank], dt_gain).astype(jnp.bfloat16)
        b_vector = rms_scale(projected[step_idx, :, dt_rank : dt_rank + state_size], b_gain)
        c_vector = rms_scale(projected[step_idx, :, dt_rank + state_size :], c_gain)
        dt_step = jax.nn.softplus(
            jnp.dot(dt_low, dt_proj_weight, preferred_element_type=jnp.float32) + dt_bias
        )
        scan_state = (
            jnp.exp(-dt_step[:, None, :] * a_rate[None]) * scan_state
            + dt_step[:, None, :] * b_vector[:, :, None] * activ[step_idx][:, None, :]
        )
        mixed = jnp.sum(c_vector[:, :, None] * scan_state, axis=1) + skip_gain * activ[step_idx]
        outputs.append(
            (mixed * jax.nn.silu(z_steps[step_idx].astype(jnp.float32))).astype(jnp.bfloat16)
        )
    return (jnp.stack(outputs), conv_rows, scan_state)


def attend_part(query_rows, key_rows, key_mask):
    head_dim = query_rows.shape[-1]
    scores = jnp.einsum(
        "snhd,nkd->snhk", query_rows, key_rows[:, :, :head_dim], preferred_element_type=jnp.float32
    ) / math.sqrt(head_dim)
    scores = jnp.where(key_mask[:, :, None, :], scores, masked_score)
    peak_score = jnp.max(scores, axis=-1)
    weights = jnp.where(key_mask[:, :, None, :], jnp.exp(scores - peak_score[..., None]), 0.0)
    weight_sum = jnp.sum(weights, axis=-1)
    weighted = jnp.einsum("snhk,nkd->snhd", weights, key_rows[:, :, head_dim:].astype(jnp.float32))
    return (peak_score, weight_sum, weighted)


def extra_allowed(count, offset, requests, step_count):
    allowed = jnp.arange(count)[None, :] <= offset + jnp.arange(step_count)[:, None]
    return jnp.broadcast_to(allowed[:, None, :], (step_count, requests, count))


def joined_mask(cache_mask, extra_mask):
    step_count = extra_mask.shape[0]
    return jnp.concatenate(
        [jnp.broadcast_to(cache_mask[None], (step_count,) + cache_mask.shape), extra_mask], axis=-1
    )


def split_attention(group_queries, key_rows, key_mask, even_rank):
    step_count, requests, head_count, head_dim = group_queries.shape
    peak_score, weight_sum, weighted = attend_part(group_queries, key_rows, key_mask)
    own_heads = head_count // 2

    def halves(values):
        lower_half = values[:, :, :own_heads]
        upper_half = values[:, :, own_heads:]
        return (
            jnp.where(even_rank, lower_half, upper_half),
            jnp.where(even_rank, upper_half, lower_half),
        )

    mine_peak, send_peak = halves(peak_score)
    mine_sum, send_sum = halves(weight_sum)
    mine_weighted, send_weighted = halves(weighted)
    far_peak, far_sum, far_weighted = swapped((send_peak, send_sum, send_weighted), "tp", 0)
    joint_peak = jnp.maximum(mine_peak, far_peak)
    own_scale = jnp.exp(mine_peak - joint_peak)
    far_scale = jnp.exp(far_peak - joint_peak)
    numer = mine_weighted * own_scale[..., None] + far_weighted * far_scale[..., None]
    denom = mine_sum * own_scale + far_sum * far_scale
    return (
        (numer / denom[..., None])
        .reshape(step_count, requests, own_heads * head_dim)
        .astype(jnp.bfloat16)
    )


def shards(
    queries,
    new_kv,
    kv_pool,
    page_table,
    kv_lengths,
    slot_source,
    mamba_x,
    mamba_z,
    conv_state,
    ssm_state,
    x_proj_weight,
    dt_proj_weight,
    dt_bias,
    a_rate,
    skip_gain,
    conv_weight,
    conv_bias,
    dt_gain,
    b_gain,
    c_gain,
):
    weights = (
        x_proj_weight,
        dt_proj_weight,
        dt_bias,
        a_rate,
        skip_gain,
        conv_weight,
        conv_bias,
        dt_gain,
        b_gain,
        c_gain,
    )
    group_count = lax.axis_size("rep")
    my_group = lax.axis_index("rep")
    parity = lax.axis_index("tp") % 2
    even_rank = parity == 0
    requests, pages_req = page_table.shape
    page_len = kv_pool.shape[2]
    head_dim = new_kv.shape[-1]
    width = 2 * head_dim
    heads_dev = queries.shape[-1] // head_dim
    step_count = queries.shape[0]
    half_steps = step_count // 2
    half_len = pages_req // 2 * page_len
    move_count = MOVE
    paired_pages = page_table.reshape(requests, pages_req // 2, 2)
    own_pages = jnp.where(even_rank, paired_pages[:, :, 0], paired_pages[:, :, 1])
    cache_half = kv_pool[:, 0][own_pages].reshape(requests, half_len, width)
    slot_pos = jnp.arange(half_len)
    half_positions = (2 * (slot_pos // page_len) + parity) * page_len + slot_pos % page_len
    old_lengths = lax.dynamic_slice_in_dim(kv_lengths, my_group * requests, requests)
    sources = lax.dynamic_slice_in_dim(slot_source, my_group * requests, requests)
    new_lengths = kv_lengths[sources]
    other_queries, other_fresh = swapped((queries, new_kv), "tp", 0)
    lower_half = jnp.where(even_rank, queries, other_queries)
    upper_half = jnp.where(even_rank, other_queries, queries)
    group_queries = jnp.concatenate([lower_half, upper_half], axis=-1).reshape(
        step_count, requests, 2 * heads_dev, head_dim
    )
    fresh_kv = jnp.concatenate(
        [jnp.where(even_rank, new_kv, other_fresh), jnp.where(even_rank, other_fresh, new_kv)],
        axis=-1,
    )
    extras = jnp.swapaxes(fresh_kv[:half_steps], 0, 1)
    key_mask = joined_mask(
        half_positions[None, :] < old_lengths[:, None],
        extra_allowed(half_steps, 0, requests, half_steps) & even_rank,
    )
    attention_first = split_attention(
        group_queries[:half_steps],
        jnp.concatenate([cache_half, extras], axis=1),
        key_mask,
        even_rank,
    )
    mixer_first, conv_mid, state_mid = mixer_steps(
        mamba_x[:half_steps], mamba_z[:half_steps], conv_state, ssm_state, weights
    )
    payload_kv = jnp.concatenate(
        [
            cache_half.reshape(requests, -1),
            extras.reshape(requests, -1),
            conv_mid.reshape(requests, -1),
        ],
        axis=1,
    )
    payload_state = state_mid.reshape(requests, -1)
    source_group = sources // requests
    source_slot = sources % requests
    foreign = source_group != my_group
    inverse = (
        jnp.zeros(group_count * requests, jnp.int32)
        .at[slot_source]
        .set(jnp.arange(group_count * requests, dtype=jnp.int32))
    )
    leaving = (
        inverse // requests != jnp.arange(group_count * requests, dtype=jnp.int32) // requests
    ).reshape(group_count, requests)
    leave_order = jnp.cumsum(leaving.astype(jnp.int32), axis=1) - 1
    picks = leaving[my_group][None, :] & (
        leave_order[my_group][None, :] == jnp.arange(move_count)[:, None]
    )
    outbox_slots = jnp.sum(jnp.where(picks, jnp.arange(requests)[None, :], 0), axis=1)
    wanted = source_group * move_count + leave_order[source_group, source_slot]

    def collect(carry, piece):
        found_here = foreign & (wanted >= 0) & (wanted < piece.shape[0])
        return jnp.where(found_here[:, None], piece[jnp.clip(wanted, 0, piece.shape[0] - 1)], carry)

    inbox_kv = collect(
        jnp.zeros_like(payload_kv),
        lax.all_gather(payload_kv[outbox_slots], "rep", axis=0, tiled=True),
    )
    inbox_state = collect(
        jnp.zeros_like(payload_state),
        lax.all_gather(payload_state[outbox_slots], "rep", axis=0, tiled=True),
    )
    moved_kv = jnp.where(foreign[:, None], inbox_kv, payload_kv[source_slot])
    moved_state = jnp.where(foreign[:, None], inbox_state, payload_state[source_slot])
    cache_cols = half_len * width
    extra_cols = half_steps * width
    cache_moved = moved_kv[:, :cache_cols].reshape(requests, half_len, width)
    old_fresh = moved_kv[:, cache_cols : cache_cols + extra_cols].reshape(
        requests, half_steps, width
    )
    conv_moved = moved_kv[:, cache_cols + extra_cols :].reshape(conv_state.shape)
    state_moved = moved_state.reshape(ssm_state.shape)
    later_extras = jnp.concatenate([old_fresh, jnp.swapaxes(fresh_kv[half_steps:], 0, 1)], axis=1)
    key_mask = joined_mask(
        half_positions[None, :] < new_lengths[:, None],
        extra_allowed(2 * half_steps, half_steps, requests, half_steps) & even_rank,
    )
    attention_second = split_attention(
        group_queries[half_steps:],
        jnp.concatenate([cache_moved, later_extras], axis=1),
        key_mask,
        even_rank,
    )
    mixer_second, conv_end, state_end = mixer_steps(
        mamba_x[half_steps:], mamba_z[half_steps:], conv_moved, state_moved, weights
    )
    attention_out = jnp.concatenate([attention_first, attention_second], axis=0)
    mixer_out = jnp.concatenate([mixer_first, mixer_second], axis=0)
    return (attention_out, mixer_out)


def solution(mesh):
    placed = (
        P(None, "rep", "tp"),
        P(None, "rep", "tp"),
        P("rep", "tp", None, None),
        P("rep", None),
        P(),
        P(),
        P(None, "rep", "tp"),
        P(None, "rep", "tp"),
        P("rep", None, "tp"),
        P("rep", None, "tp"),
        P(None, "tp"),
        P(None, "tp"),
        P("tp"),
        P(None, "tp"),
        P("tp"),
        P(None, "tp"),
        P("tp"),
        P(),
        P(),
        P(),
    )
    return jax.shard_map(
        shards,
        mesh=mesh,
        in_specs=placed,
        out_specs=(P(None, "rep", "tp"), P(None, "rep", "tp")),
        check_vma=False,
    )
```

profile of v0, /device:TPU:8, one launch (start us, length us, event | category | flops | bytes accessed | tf_op | source)
XLA Modules:
  0.0 764.7 jit_solution(9126022795161117182)
XLA Ops:
  7.2 0.8 copy.69
  8.1 1.9 collective-permute-start
  10.0 0.7 compare_select_fusion.5
  10.7 0.8 compare_select_fusion.10
  11.5 2.4 scatter_custom_fusion
  14.0 0.8 compare_select_fusion.4
  15.3 1.0 copy.72
  16.3 0.8 slice_bitcast_fusion.9
  17.9 0.8 copy-done.3
  19.7 0.6 fusion.66
  20.4 1.3 gather_fusion.2
  21.7 0.8 fusion.91
  22.5 0.7 gather_fusion.1
  23.4 1.0 gather_fusion.4
  24.4 226.9 %all-gather.7.cloned.1.call-done = bf16[32,2,19968]{2,1,0:T(2,128)(2,1)} async-done(((bf16[1,2,19968]{2,1,0:T(2,128)(2,1)}), bf16[32,2,19968]{2,1,0:T(2,128)(2,1)}) %all-gather.7.cloned.1.call-update) | async-done | bytes 2555920 | tf_op jit(solution)/shard_map/all_gather | solution.py:235
  251.3 4.4 reshape.1098
  255.7 3.5 gather_fusion.3
  259.4 0.8 copy-done.7
  260.6 1.1 multiply_reduce_fusion.4
  261.8 1.1 fusion.4
  262.9 1.1 fusion.6
  264.0 0.7 divide_multiply_fusion
  264.8 243.3 %all-reduce.3.cloned.1.call-done = (f32[2,16,544]{2,1,0:T(8,128)}, f32[2,16,544]{2,1,0:T(8,128)}) async-done(((f32[2,16,544]{2,1,0:T(8,128)}, f32[2,16,544]{2,1,0:T(8,128)}), (f32[2,16,544]{2,1,0:T(8,128)}, f32[2,16,544]{2,1,0:T(8,128)})) %all-reduce.3.cloned.1.call-update) | async-done | bytes 139280 | tf_op jit(solution)/shard_map/psum | solution.py:49
  508.1 0.9 multiply_reduce_fusion.11
  509.1 1.0 multiply_reduce_fusion.19
  510.2 1.0 multiply_reduce_fusion.15
  511.3 1.2 fusion.106
  512.8 1.5 multiply_multiply_fusion.1
  514.3 1.5 multiply_reduce_fusion.2
  516.4 1.3 gather_fusion.6
  517.7 1.9 collective-permute-start.1
  520.3 1.2 gather_fusion.5
  521.5 0.8 broadcast_compare_fusion.1
  522.5 0.7 pad_add_fusion.1
  523.2 0.9 broadcast_select_fusion.1
  524.1 1.3 fusion.104
  525.5 2.4 collective-permute-start.2
  528.2 1.9 collective-permute-start.4
  530.5 0.6 copy.90
  531.1 2.4 collective-permute-start.3
  533.6 0.7 collective-permute-done.3
  534.4 0.8 fusion.56
  535.2 1.4 convert_element_type.76
  536.5 1.4 copy.76
  537.9 1.9 slice.248
  540.4 1.2 copy.89
  541.6 0.8 pad_maximum_fusion
  542.8 2.3 collective-permute-start.5
  545.4 2.1 collective-permute-start.7
  547.8 2.2 collective-permute-start.6
  550.2 0.8 collective-permute-done.6
  551.0 0.8 fusion.57
  551.7 1.4 convert_element_type.79
  553.1 0.8 copy.77
  553.9 1.4 pad_maximum_fusion.7
  555.3 1.9 gather_fusion.8
  557.2 1.9 copy.93
  559.3 1.0 fusion.107
  560.2 1.0 fusion.108
  561.2 183.0 %all-gather.9.cloned.1.call-done = f32[32,2,16384]{2,1,0:T(2,128)} async-done(((f32[1,2,16384]{2,1,0:T(2,128)}), f32[32,2,16384]{2,1,0:T(2,128)}) %all-gather.9.cloned.1.call-update) | async-done | bytes 4194320 | tf_op jit(solution)/shard_map/all_gather | solution.py:239
  744.2 6.1 reshape.1100
  750.4 3.7 gather_fusion.7
  755.4 1.8 multiply_reduce_fusion.1
  757.5 0.7 pad_maximum_fusion.5
  (198 shorter events, 9.0 us)
Async XLA Ops:
  7.2 254.6 %copy-start = (bf16[544,1024]{1,0:T(8,128)(2,1)S(1)}, bf16[544,1024]{1,0:T(8,128)(2,1)}, u32[]{:S(2)}) copy-start(bf16[544,1024]{1,0:T(8,128)(2,1)} %param.30) | copy-start | bytes 3342340
  7.2 10.1 %copy-start.12 = (bf16[64,1,16,256]{3,2,1,0:T(8,128)(2,1)S(1)}, bf16[64,1,16,256]{3,2,1,0:T(8,128)(2,1)}, u32[]{:S(2)}) copy-start(bf16[64,1,16,256]{3,2,1,0:T(8,128)(2,1)} %param.22) | copy-start | bytes 1572868
  7.2 244.1 %all-gather.7.cloned.1.call-start = ((), (), s32[]{:S(2)}) async-start(), calls=%async_computation | async-start | bytes 2635776 | tf_op jit(solution)/shard_map/all_gather | solution.py:235
  8.1 11.4 %collective-permute-start = (bf16[4,16,128]{2,0,1:T(4,128)(2,1)S(1)}, bf16[4,16,128]{2,0,1:T(4,128)(2,1)S(1)}, u32[]{:S(2)}, u32[]{:S(2)}) collective-permute-start(bf16[4,16,128]{2,0,1:T(4,128)(2,1)S(1)} %copy.69), channel_id=1, source_target_pairs={{0,1},{1,0},{2,3},{3,2},{4,5},{5,4},{6,7},{7,6},{8,9},{9,8},{10,11... | collective-permute-start | bytes 49160 | tf_op jit(solution)/shard_map/ppermute | solution.py:16
  17.9 0.8 copy-start.3
  20.3 1.4 copy-start.24
  21.7 486.5 %all-reduce.3.cloned.1.call-start = ((), (), s32[]{:S(2)}) async-start(), calls=%async_computation.2 | async-start | bytes 327680 | tf_op jit(solution)/shard_map/psum | solution.py:49
  23.3 1.1 copy-start.45
  23.3 232.3 %copy-start.44 = (s32[1024]{0:T(1024)}, s32[1024]{0:T(1024)S(1)}, u32[]{:S(2)}) copy-start(s32[1024]{0:T(1024)S(1)} %pad_clamp_fusion.2) | copy-start | bytes 12292
  23.4 235.9 %copy-start.46 = (pred[16]{0:T(512)(128)(4,1)}, pred[16]{0:T(512)(128)(4,1)S(1)}, u32[]{:S(2)}) copy-start(pred[16]{0:T(512)(128)(4,1)S(1)} %get-tuple-element.31) | copy-start | bytes 52
  23.4 235.9 %copy-start.48 = (pred[16]{0:T(512)(128)(4,1)}, pred[16]{0:T(512)(128)(4,1)S(1)}, u32[]{:S(2)}) copy-start(pred[16]{0:T(512)(128)(4,1)S(1)} %get-tuple-element.32) | copy-start | bytes 52
  259.2 1.3 copy-start.43
  259.4 0.8 copy-start.7
  260.2 1.5 copy-start.33
  262.9 248.3 %copy-start.2 = (bf16[512,1024]{1,0:T(8,128)(2,1)S(1)}, bf16[512,1024]{1,0:T(8,128)(2,1)}, u32[]{:S(2)}) copy-start(bf16[512,1024]{1,0:T(8,128)(2,1)} %param.31) | copy-start | bytes 3145732
  262.9 248.3 %copy-start.29 = (f32[1024]{0:T(1024)S(1)}, f32[1024]{0:T(1024)}, u32[]{:S(2)}) copy-start(f32[1024]{0:T(1024)} %param.32) | copy-start | bytes 12292
  262.9 248.3 %copy-start.35 = (f32[512]{0:T(512)S(1)}, f32[512]{0:T(512)}, u32[]{:S(2)}) copy-start(f32[512]{0:T(512)} %param.37) | copy-start | bytes 6148
  264.0 480.3 %all-gather.9.cloned.1.call-start = ((), (), s32[]{:S(2)}) async-start(), calls=%async_computation.1 | async-start | bytes 4325376 | tf_op jit(solution)/shard_map/all_gather | solution.py:239
  264.8 249.5 %copy-start.10 = (f32[16,1024]{1,0:T(8,128)}, f32[16,1024]{1,0:T(8,128)S(1)}, u32[]{:S(2)}) copy-start(f32[16,1024]{1,0:T(8,128)S(1)} %get-tuple-element.67) | copy-start | bytes 196612
  508.1 4.3 copy-start.14
  511.2 1.5 copy-start.51
  511.2 1.5 copy-start.52
  511.3 3.0 copy-start.5
  511.3 3.0 copy-start.15
  512.8 3.0 copy-start.8
  514.3 1.5 copy-start.27
  516.4 3.3 copy-start.1
  517.7 5.4 collective-permute-start.1
  521.5 8.7 %copy-start.4 = (bf16[64,16,256]{2,1,0:T(8,128)(2,1)S(1)}, bf16[64,16,256]{2,1,0:T(8,128)(2,1)}, u32[]{:S(2)}) copy-start(bf16[64,16,256]{2,1,0:T(8,128)(2,1)} %copy-done.3) | copy-start | bytes 1572868
  521.5 8.7 %copy-start.25 = (bf16[2,16,256]{2,0,1:T(2,128)(2,1)S(1)}, bf16[2,16,256]{2,0,1:T(2,128)(2,1)}, u32[]{:S(2)}) copy-start(bf16[2,16,256]{2,0,1:T(2,128)(2,1)} %copy-done.24) | copy-start | bytes 49156
  525.5 8.0 %collective-permute-start.2 = (f32[2,16,4]{2,0,1:T(2,128)S(1)}, f32[2,16,4]{2,0,1:T(2,128)S(1)}, u32[]{:S(2)}, u32[]{:S(2)}) collective-permute-start(f32[2,16,4]{2,0,1:T(2,128)S(1)} %broadcast_select_fusion.6), channel_id=1, source_target_pairs={{0,1},{1,0},{2,3},{3,2},{4,5},{5,4},{6,7},{7,6},{8,9},{9,8},{10,11... | collective-permute-start | bytes 1544 | tf_op jit(solution)/shard_map/ppermute | solution.py:16
  528.2 5.3 collective-permute-start.4
  530.4 9.3 %slice-start = ((bf16[16,19968]{1,0:T(8,128)(2,1)}), bf16[16,512]{1,0:T(8,128)(2,1)S(1)}, s32[]{:S(2)}) async-start(bf16[16,19968]{1,0:T(8,128)(2,1)} %copy-done.7), calls=%async_computation.3 | async-start | bytes 32768 | tf_op jit(solution)/shard_map/slice | solution.py:246
  531.1 3.3 collective-permute-start.3
  540.4 2.0 copy-start.31
  540.4 2.0 copy-start.42
  542.8 7.2 collective-permute-start.5
  545.4 4.6 collective-permute-start.7
  547.8 3.1 collective-permute-start.6
  557.2 1.9 copy-start.13
  557.2 2.0 copy-start.30
  557.2 2.0 copy-start.36
  754.0 1.2 copy-start.6
  754.0 1.2 copy-start.9
  754.0 1.2 copy-start.11
  754.1 1.2 copy-start.16
  754.1 1.2 copy-start.17
  754.1 1.2 copy-start.18
  754.1 1.2 copy-start.19
  754.1 1.2 copy-start.20
  754.1 1.2 copy-start.21
  754.1 1.2 copy-start.22
  754.1 1.2 copy-start.28
  754.1 1.2 copy-start.37
  754.1 1.2 copy-start.38
  754.2 1.2 copy-start.39
  754.2 1.2 copy-start.40
  754.2 1.2 copy-start.41
  754.2 1.2 copy-start.47
  754.2 1.2 copy-start.49
  755.4 1.9 copy-start.23
  755.4 1.9 copy-start.26
  755.4 1.9 copy-start.34
  755.4 1.9 copy-start.50
  (1 other events, 0.7 us)
Sparse Core Ops, SparseCore 0:
  21.8 229.4 all-gather.6
  264.1 243.9 all-reduce.2
  517.9 226.3 all-gather.8
where the time goes:
time: 766 us; the launch traced here: 765 us
  waiting for transfers between devices  655 us (86%)
  local copies, waits for them, and re-layouts  47.2 us (6%)
  other arithmetic  22.6 us (3%)
  starting transfers between devices  17.3 us (2%)
  between operations  15 us (2%)
  matrix products  7.79 us (1%)
    psum x1, waiting for transfers between devices, mixer_steps(): projected = lax.psum(partial_terms, 'tp')  243 us
    all_gather x1, waiting for transfers between devices, shards(): lax.all_gather(payload_kv[outbox_slots], 'rep', axis=0, tiled=True)  227 us
    all_gather x1, waiting for transfers between devices, shards(): lax.all_gather(payload_state[outbox_slots], 'rep', axis=0, tiled=True)  183 us
    unnamed x120, local copies, waits for them, and re-layouts  19.9 us
    ppermute x8, starting transfers between devices, swapped(): lax.ppermute(value, axis, [(i, i ^ 1 << distance) for i in range(lax.axis...  17.1 us
  transfers between devices with their start and end apart: 11, of which 5 were waited for; matrix products, arithmetic and copies ran while one was open for 5% of the time, Pallas kernels for 0%

commit v1 on v0

v1 whole, which is shorter than its diff:
```python
import functools

import jax
import jax.numpy as jnp
from jax import lax
from jax.experimental import pallas as pl
from jax.experimental.pallas import tpu as pltpu
from jax.sharding import PartitionSpec as P

F32 = jnp.float32
BF16 = jnp.bfloat16
I32 = jnp.int32
EPS = 1e-06
MASKED = -1e30
SCALE = 128**-0.5


def geometry(mesh):
    rep, tp = mesh.shape["rep"], mesh.shape["tp"]
    ny = 4 if rep >= 16 else 2
    return (rep // ny, ny, tp // 4)


def nn(a, b):
    return lax.dot_general(a, b, (((1,), (0,)), ((), ())), preferred_element_type=F32)


def nt(a, b):
    return lax.dot_general(a, b, (((1,), (1,)), ((), ())), preferred_element_type=F32)


def hot(cond):
    return jnp.where(cond, 1.0, 0.0).astype(BF16)


def iota(shape, dim):
    return lax.broadcasted_iota(I32, shape, dim)


def silu(v):
    return v / (1.0 + jnp.exp(-v))


def softplus(v):
    return jnp.maximum(v, 0.0) + jnp.log1p(jnp.exp(-jnp.abs(v)))


def attend(q_rows, keys, values, extra_keys, extra_values, bias, extra_bias):
    scores = nt(q_rows, keys) * SCALE + bias
    extra = nt(q_rows, extra_keys) * SCALE + extra_bias
    peak = jnp.maximum(
        jnp.max(scores, axis=1, keepdims=True), jnp.max(extra, axis=1, keepdims=True)
    )
    weight = jnp.exp(scores - peak)
    extra_weight = jnp.exp(extra - peak)
    total = jnp.sum(weight, axis=1, keepdims=True) + jnp.sum(extra_weight, axis=1, keepdims=True)
    out = nn(weight.astype(BF16), values) + nn(extra_weight.astype(BF16), extra_values)
    lane = iota((q_rows.shape[0], 128), 1)
    return out, jnp.where(lane < 64, peak, total)


def combine(near, far):
    near_peak, near_sum = near[:, 128:129], near[:, 192:193]
    far_peak, far_sum = far[:, 128:129], far[:, 192:193]
    peak = jnp.maximum(near_peak, far_peak)
    near_scale = jnp.exp(near_peak - peak)
    far_scale = jnp.exp(far_peak - peak)
    numer = near[:, :128] * near_scale + far[:, :128] * far_scale
    return numer / (near_sum * near_scale + far_sum * far_scale)


def tail_norm(tail):
    lane = iota(tail.shape, 1)
    square = tail * tail
    mean_b = jnp.sum(jnp.where(lane < 16, square, 0.0), axis=1, keepdims=True) / 16.0
    mean_c = jnp.sum(
        jnp.where((lane >= 16) & (lane < 32), square, 0.0), axis=1, keepdims=True
    ) / 16.0
    scale = jnp.where(lane < 16, lax.rsqrt(mean_b + EPS), lax.rsqrt(mean_c + EPS))
    return jnp.where(lane < 32, tail * scale, 0.0)


def by_quarter(blocks):
    quarter = iota(blocks[0].shape, 0) >> 2
    return jnp.where(
        quarter == 0,
        blocks[0],
        jnp.where(quarter == 1, blocks[1], jnp.where(quarter == 2, blocks[2], blocks[3])),
    )


def kernel(
    geo,
    src_s,
    src_ref,
    len_ref,
    page_ref,
    q_ref,
    nk_ref,
    x_ref,
    z_ref,
    conv_ref,
    dtb_ref,
    a_ref,
    skip_ref,
    cw_ref,
    cb_ref,
    dtg_ref,
    bg_ref,
    cg_ref,
    pool_hbm,
    ssm_hbm,
    xw_hbm,
    dw_hbm,
    attn_ref,
    mix_ref,
    pool,
    ssm,
    xw,
    dw,
    mid,
    act,
    dts,
    mixed,
    dtl,
    tails,
    gather_in,
    stage_y,
    land_y,
    land_o,
    q_other,
    nk_other,
    part,
    part_land,
    half_send,
    half_land,
    norm_send,
    norm_land,
    near,
    away,
    far,
    late_send,
    late_land,
    late_half,
    late_half_land,
    late_away,
    late_far,
    gather_out,
    stage_r,
    land_r,
    bias_ref,
    mask_ref,
    ssem,
    rsem,
    lsem,
):
    nz, ny, nx = geo
    no = 2 * nx
    rpo = 64 // no
    n = src_ref.shape[1]
    rep, tp = lax.axis_index("rep"), lax.axis_index("tp")
    zi, yi = rep // ny, rep % ny
    core, zh, xi = tp % 2, (tp // 2) % 2, tp // 4
    own = xi * 2 + core
    tp_other = tp + 1 - 2 * core
    tp_half = tp + 2 - 4 * zh

    def o_tp(d):
        o = (own + d) % no
        return (o // 2) * 4 + zh * 2 + o % 2

    def z_rep(d):
        return ((zi + d) % nz) * ny + yi

    def y_rep(e):
        return zi * ny + (yi + e) % ny

    partners = [(z_rep(d), tp) for d in range(1, nz)]
    partners += [(y_rep(e), tp) for e in range(1, ny)]
    partners += [(y_rep(e), tp_other) for e in range(1, ny)]
    partners += [(rep, o_tp(d)) for d in range(1, no)]
    partners += [(rep, tp_half)]
    barrier = pltpu.get_barrier_semaphore()
    for device in partners:
        pl.semaphore_signal(
            barrier, inc=1, device_id=device, device_id_type=pl.DeviceIdType.MESH
        )

    loads = []
    for k, (a, b) in enumerate(((xw_hbm, xw), (pool_hbm, pool), (dw_hbm, dw), (ssm_hbm, ssm))):
        load = pltpu.make_async_copy(a, b, lsem.at[k])
        load.start()
        loads.append(load)

    used = []

    def push(src, dst, device):
        k = len(used)
        copy = pltpu.make_async_remote_copy(
            src_ref=src,
            dst_ref=dst,
            send_sem=ssem.at[k],
            recv_sem=rsem.at[k],
            device_id=device,
            device_id_type=pl.DeviceIdType.MESH,
        )
        copy.start()
        used.append(copy)
        return copy

    src = src_ref[...]
    lane_n = iota((1, n), 1)
    foreign = src != lane_n
    foreign16 = jnp.broadcast_to(hot(foreign), (16, n))
    slot_pick = hot(iota((128, n), 1) == rep * 16 + (iota((128, n), 0) & 15))
    f128 = nt(foreign16, slot_pick)
    before = hot(
        (iota((128, 128), 0) < 16) & (iota((128, 128), 0) < (iota((128, 128), 1) & 15))
    )
    k128 = nn(f128.astype(BF16), before)
    row = iota((16, 128), 0)
    col = iota((16, 128), 1)
    rank = ((row >> 1) & 1).astype(F32)
    place = (f128 > 0.5) & (k128 == rank)
    pack = hot(place & ((row >> 2) == ((col >> 4) & 3)) & ((row & 1) == (col >> 6)))
    pick16 = hot(place & (col < 16))[:, :16]

    blocks = []
    nothing = jnp.zeros((16, 256), BF16)
    for s in (2, 3):
        x_s = x_ref[s]
        q_s = q_ref[s]
        nk_s = nk_ref[s]
        for b in range(4):
            side = (
                q_s[:, b * 256 : (b + 1) * 256]
                if b < 2
                else (jnp.concatenate([nk_s, nothing[:, :128]], axis=1) if b == 2 else nothing)
            )
            blocks.append(jnp.concatenate([x_s[:, b * 256 : (b + 1) * 256], side], axis=1))
    gather_in[0] = nn(pack, jnp.concatenate(blocks, axis=0)).astype(BF16)

    pl.semaphore_wait(barrier, len(partners))

    z_in = [push(gather_in.at[0], gather_in.at[d], (z_rep(d), tp)) for d in range(1, nz)]
    q_swap = push(q_ref, q_other, (rep, tp_other))
    nk_swap = push(nk_ref, nk_other, (rep, tp_other))

    conv = conv_ref[...].astype(F32)
    window = [conv[:, w, :] for w in range(3)] + [x_ref[s].astype(F32) for s in range(4)]
    conv_last = window[2].astype(BF16)
    cw = cw_ref[...]
    cb = cb_ref[...]
    activ = []
    for s in range(4):
        total = window[s] * cw[0:1]
        for w in range(1, 4):
            total = total + window[s + w] * cw[w : w + 1]
        activ.append(silu(total + cb))
        act[s] = activ[s]
    activ_b = jnp.concatenate([v.astype(BF16) for v in activ], axis=0)
    loads[0].wait()

    def project(rows):
        tail = jnp.concatenate([xw[512:544, :], jnp.zeros((96, 1024), BF16)], axis=0)
        return nt(rows, xw[0:512, :]), nt(rows, tail)

    main, tail = project(activ_b)
    for o in range(no):
        part[o, :, 0:512] = main[o * rpo : (o + 1) * rpo]
        part[o, :, 512:640] = tail[o * rpo : (o + 1) * rpo]
    part_out = [
        push(part.at[(own + d) % no], part_land.at[d], (rep, o_tp(d))) for d in range(1, no)
    ]

    same = iota((n, n), 0)
    lane_nn = iota((n, n), 1)
    rank16 = nn(foreign16, hot(((same >> 4) == (lane_nn >> 4)) & (same < lane_nn)))
    rank_there = nn(rank16.astype(BF16), hot(same == src))
    home = jnp.where(foreign, (lane_n >> 4) * 2 + rank16[0:1].astype(I32), -1)
    donor = jnp.where(foreign, (src >> 4) * 2 + rank_there[0:1].astype(I32), -1)
    to_row = iota((ny * 16, n), 0)
    to_code = (zi * ny + ((yi + (to_row >> 4)) & (ny - 1))) * 2 + ((to_row >> 1) & 1)
    from_row = iota((nz * 16, n), 0)
    from_code = (((zi - (from_row >> 4)) & (nz - 1)) * ny + yi) * 2 + ((from_row >> 1) & 1)
    r_ = iota((ny * 16, nz * 16), 0)
    c_ = iota((ny * 16, nz * 16), 1)
    alike = ((r_ >> 2) & 3 == (c_ >> 2) & 3) & ((r_ & 1) == (c_ & 1))
    select_in = hot(alike & (nt(hot(donor == to_code), hot(home == from_code)) > 0.5))
    select_out = hot(alike & (nt(hot(home == to_code), hot(donor == from_code)) > 0.5))

    own_lane = iota((16, n), 1) == rep * 16 + iota((16, n), 0)
    lengths = jnp.sum(jnp.where(own_lane, len_ref[...], 0), axis=1, keepdims=True)
    foreign_col = (
        jnp.sum(jnp.where(own_lane & foreign, 1.0, 0.0), axis=1, keepdims=True) > 0.5
    )
    table = page_ref[...]
    cache_lane = iota((16, 1024), 1)
    allowed = jnp.zeros((16, 1024), F32)
    for k in range(4):
        page = jnp.where(core == 0, table[:, 2 * k : 2 * k + 1], table[:, 2 * k + 1 : 2 * k + 2])
        limit = lengths - (2 * k + core) * 16
        allowed = jnp.where(
            ((cache_lane >> 4) == page) & ((cache_lane & 15) < limit), 1.0, allowed
        )
    mask_ref[...] = allowed.astype(BF16)
    bias_ref[...] = jnp.where(allowed > 0.5, 0.0, MASKED)

    for copy in z_in:
        copy.wait_recv()
    chosen = nn(select_in, gather_in[...].reshape(nz * 16, 512)).astype(BF16)
    for e in range(ny):
        stage_y[e] = chosen[e * 16 : (e + 1) * 16]
    land_y[0] = chosen[0:16]
    y_in = [push(stage_y.at[e], land_y.at[e], (y_rep(e), tp)) for e in range(1, ny)]
    y_in += [
        push(stage_y.at[e, :, 256:512], land_o.at[e], (y_rep(e), tp_other)) for e in range(ny)
    ]

    for copy in part_out:
        copy.wait_recv()
    summed = part[own]
    for d in range(1, no):
        summed = summed + part_land[d]
    blank = jnp.zeros((rpo, 128), F32)

    def pack_half(v):
        return jnp.concatenate(
            [
                jnp.concatenate([v[:, 0:256], v[:, 512:640]], axis=1),
                jnp.concatenate([v[:, 256:512], blank], axis=1),
            ],
            axis=0,
        ).astype(BF16)

    def unpack_half(v):
        v = v.astype(F32)
        return jnp.concatenate([v[:rpo, 0:256], v[rpo:, 0:256], v[:rpo, 256:384]], axis=1)

    half_send[...] = pack_half(summed)
    half = push(half_send, half_land, (rep, tp_half))

    loads[1].wait()
    q_swap.wait_recv()
    nk_swap.wait_recv()
    pages = pool[...].reshape(1024, 256)
    keys, values = pages[:, 0:128], pages[:, 128:256]
    pad64 = jnp.zeros((64, 128), BF16)
    new_keys = [nk_ref[s] for s in range(4)]
    new_values = [nk_other[s] for s in range(4)]
    extra_keys = jnp.concatenate(new_keys + [pad64], axis=0)
    extra_values = jnp.concatenate(new_values + [pad64], axis=0)
    row_q = iota((256, 128), 0)
    col_q = iota((256, 128), 1)
    extra_bias = jnp.where(
        ((row_q & 15) == (col_q & 15)) & ((col_q >> 4) <= (row_q >> 6)) & (core == 0), 0.0, MASKED
    )
    bias16 = bias_ref[...]
    bias = jnp.concatenate([bias16] * 16, axis=0)
    for source, target in ((q_other, away), (q_ref, near)):
        rows = jnp.concatenate(
            [source[s][:, h * 128 : (h + 1) * 128] for s in range(4) for h in range(4)], axis=0
        )
        out, stats = attend(rows, keys, values, extra_keys, extra_values, bias, extra_bias)
        target[:, 0:128] = out
        target[:, 128:256] = stats
        if target is away:
            partial = push(away, far, (rep, tp_other))

    for copy in y_in:
        copy.wait_recv()
    er = iota((128, ny * 16), 0)
    ec = iota((128, ny * 16), 1)
    wanted_step = jnp.where(er < 64, er & 1, 0)
    expand = hot(
        (((er >> 4) & 3) == ((ec >> 2) & 3))
        & (((er >> 1) & 1) == ((ec >> 1) & 1))
        & (wanted_step == (ec & 1))
    )
    arrived = nn(expand, land_y[...].reshape(ny * 16, 512))
    arrived_o = nn(expand[0:64], land_o[...].reshape(ny * 16, 256))
    x_now = jnp.concatenate([arrived[b * 16 : (b + 1) * 16, 0:256] for b in range(4)], axis=1)
    x_prev = jnp.concatenate(
        [arrived[64 + b * 16 : 64 + (b + 1) * 16, 0:256] for b in range(4)], axis=1
    )
    last_row = nn(pick16, conv_last)
    x_zero = nn(pick16, x_ref[0])
    x_one = nn(pick16, x_ref[1])
    odd = (iota((16, 1024), 0) & 1) == 1
    total = jnp.where(odd, x_zero, last_row) * cw[0:1]
    total = total + jnp.where(odd, x_one, x_zero) * cw[1:2]
    total = total + jnp.where(odd, x_prev, x_one) * cw[2:3]
    total = total + x_now * cw[3:4]
    late_act = silu(total + cb)
    main, tail = project(late_act.astype(BF16))
    late_own = jnp.concatenate(
        [by_quarter([main[:, b * 128 : (b + 1) * 128] for b in range(4)]), tail], axis=1
    )
    late_send[...] = late_own.astype(BF16)
    late_out = [push(late_send, late_land.at[d], (rep, o_tp(d))) for d in range(1, no)]

    half.wait_recv()
    summed = summed + unpack_half(half_land[...])
    main = summed[:, 0:512]
    mean = jnp.sum(main * main, axis=1, keepdims=True) / 512.0
    low = main * lax.rsqrt(mean + EPS) * dtg_ref[...]
    normed = jnp.concatenate([low, tail_norm(summed[:, 512:640])], axis=1)
    packed = pack_half(normed)
    norm_send[...] = packed
    norm_out = [push(norm_send, norm_land.at[d], (rep, o_tp(d))) for d in range(1, no)]

    def take(o, v):
        v = unpack_half(v)
        start = pl.multiple_of(o * rpo, rpo)
        dtl[pl.ds(start, rpo), :] = v[:, 0:512]
        tails[pl.ds(start, rpo), :] = v[:, 512:640]

    take(own, packed)

    q_late = jnp.concatenate(
        [
            v[(h // 2) * 16 : (h // 2) * 16 + 8, off + (h % 2) * 128 : off + (h % 2) * 128 + 128]
            for v, off in ((arrived, 256), (arrived_o, 0))
            for h in range(4)
        ],
        axis=0,
    ).astype(BF16)
    pad48 = jnp.zeros((48, 128), BF16)
    late_keys = jnp.concatenate(
        new_keys + [arrived[32:48, 256:384].astype(BF16), pad48], axis=0
    )
    late_values = jnp.concatenate(
        new_values + [arrived_o[32:48, 0:128].astype(BF16), pad48], axis=0
    )
    fits = (place & (col < 32)) | (
        (col >= 64)
        & (col < 68)
        & (((col >> 1) & 1) == ((row >> 1) & 1))
        & ((col & 1) <= (row & 1))
    )
    late_extra = jnp.where(fits & (core == 0), 0.0, MASKED)[0:8]
    late_bias = jnp.where(nn(pick16, mask_ref[...]) > 0.5, 0.0, MASKED)[0:8]
    out, stats = attend(
        q_late,
        keys,
        values,
        late_keys,
        late_values,
        jnp.concatenate([late_bias] * 8, axis=0),
        jnp.concatenate([late_extra] * 8, axis=0),
    )
    late_near = jnp.concatenate([out[0:32], stats[0:32]], axis=1)
    late_away[...] = jnp.concatenate([out[32:64], stats[32:64]], axis=1)
    late_partial = push(late_away, late_far, (rep, tp_other))

    for copy in late_out:
        copy.wait_recv()
    late_sum = late_own
    for d in range(1, no):
        late_sum = late_sum + late_land[d].astype(F32)
    late_half[...] = late_sum.astype(BF16)
    late_swap = push(late_half, late_half_land, (rep, tp_half))

    for d, copy in enumerate(norm_out, 1):
        copy.wait_recv()
        take((own - d + no) % no, norm_land[d])
    loads[2].wait()
    steps = softplus(nn(dtl[...].astype(BF16), dw[...]) + dtb_ref[...])
    for s in range(4):
        dts[s] = steps[s * 16 : (s + 1) * 16]
    eye = iota((16, 16), 0) == iota((16, 16), 1)
    b_gain = jnp.sum(jnp.where(eye, bg_ref[...], 0.0), axis=1, keepdims=True)
    c_gain = jnp.sum(jnp.where(eye, cg_ref[...], 0.0), axis=1, keepdims=True)
    skip = skip_ref[...]
    loads[3].wait()

    def columns(tail_row):
        b = jnp.sum(jnp.where(col == row, tail_row, 0.0), axis=1, keepdims=True) * b_gain
        c = jnp.sum(jnp.where(col == row + 16, tail_row, 0.0), axis=1, keepdims=True) * c_gain
        return b, c

    def advance(state, dt_row, act_row, tail_row):
        b, c = columns(tail_row)
        state = jnp.exp(-dt_row * a_ref[...]) * state + (dt_row * act_row) * b
        return state, jnp.sum(state * c, axis=0, keepdims=True) + skip * act_row

    def scan(first, held, keep):
        def body(i, carry):
            state = held[i]
            for s in (first, first + 1):
                state, out = advance(
                    state,
                    dts[s, pl.ds(i, 1), :],
                    act[s, pl.ds(i, 1), :],
                    tails[pl.ds(s * 16 + i, 1), :],
                )
                mixed[s, pl.ds(i, 1), :] = out
            if keep:
                mid[i] = state
            return carry

        lax.fori_loop(0, 16, body, 0)

    scan(0, ssm, True)

    late_swap.wait_recv()
    late_sum = late_sum + late_half_land[...].astype(F32)
    main = late_sum[:, 0:128]
    square = jnp.broadcast_to(jnp.sum(main * main, axis=1, keepdims=True), (16, 128))
    square = square + pltpu.roll(square, 8, 0)
    square = square + pltpu.roll(square, 4, 0)
    gain = dtg_ref[...]
    gains = by_quarter(
        [jnp.broadcast_to(gain[:, b * 128 : (b + 1) * 128], (16, 128)) for b in range(4)]
    )
    low = (main * lax.rsqrt(square / 512.0 + EPS) * gains).astype(BF16)
    wr = iota((64, 16), 0)
    wc = iota((64, 16), 1)
    spread = nn(hot(((wr >> 4) == (wc >> 2)) & ((wr & 3) == (wc & 3))), low)
    low = jnp.concatenate([spread[b * 16 : (b + 1) * 16] for b in range(4)], axis=1)
    late_dt = softplus(nn(low.astype(BF16), dw[...]) + dtb_ref[...])
    late_tail = tail_norm(late_sum[:, 128:256])

    base = rep * 16
    first = jnp.int32(-1)
    second = jnp.int32(0)
    for i in range(16):
        moves = src_s[base + i] != base + i
        second = jnp.where(moves & (first >= 0), i, second)
        first = jnp.where(moves & (first < 0), i, first)
    first = jnp.maximum(first, 0)
    rows = iota((16, 1024), 0) & 3
    late_mixed = jnp.zeros((16, 1024), F32)
    for r, slot in enumerate((first, second)):
        state = mid[slot]
        for s in range(2):
            m = r * 2 + s
            state, out = advance(
                state, late_dt[m : m + 1], late_act[m : m + 1], late_tail[m : m + 1]
            )
            late_mixed = jnp.where(rows == m, out, late_mixed)
    late_partial.wait_recv()
    heads = combine(late_near, late_far[...]).astype(BF16)
    hr = iota((16, 32), 0)
    hc = iota((16, 32), 1)
    heads = nn(hot(((hr >> 2) == (hc >> 3)) & ((hr & 3) == (hc & 7))), heads)
    quarter = by_quarter([late_mixed[:, b * 256 : (b + 1) * 256] for b in range(4)])
    gather_out[0] = jnp.concatenate([quarter, heads], axis=1).astype(BF16)
    z_out = [push(gather_out.at[0], gather_out.at[d], (z_rep(d), tp)) for d in range(1, nz)]

    scan(2, mid, False)
    partial.wait_recv()
    kept = []
    for s in range(4):
        block = combine(near[s * 64 : (s + 1) * 64, :], far[s * 64 : (s + 1) * 64, :])
        block = jnp.concatenate([block[h * 16 : (h + 1) * 16] for h in range(4)], axis=1)
        if s < 2:
            attn_ref[s] = block.astype(BF16)
            mix_ref[s] = (mixed[s] * silu(z_ref[s].astype(F32))).astype(BF16)
        else:
            kept.append(block)

    for copy in z_out:
        copy.wait_recv()
    chosen = nn(select_out, gather_out[...].reshape(nz * 16, 384)).astype(BF16)
    for e in range(ny):
        stage_r[e] = chosen[e * 16 : (e + 1) * 16]
    land_r[0] = chosen[0:16]
    y_out = [push(stage_r.at[e], land_r.at[e], (y_rep(e), tp)) for e in range(1, ny)]
    own_code = rep * 2 + ((iota((ny * 16, n), 0) >> 1) & 1)
    fr = iota((128, ny * 16), 0)
    fc = iota((128, ny * 16), 1)
    put = hot(
        (((fr >> 4) & 3) == ((fc >> 2) & 3))
        & ((fr >> 6) == (fc & 1))
        & (nt(slot_pick, hot(home == own_code)) > 0.5)
    )
    for copy in y_out:
        copy.wait_recv()
    returned = nn(put, land_r[...].reshape(ny * 16, 384))
    for s in (2, 3):
        pieces = [returned[(s - 2) * 64 + b * 16 : (s - 2) * 64 + b * 16 + 16] for b in range(4)]
        back = jnp.concatenate([v[:, 0:256] for v in pieces], axis=1)
        whole = jnp.where(foreign_col, back, mixed[s])
        mix_ref[s] = (whole * silu(z_ref[s].astype(F32))).astype(BF16)
        back = jnp.concatenate([v[:, 256:384] for v in pieces], axis=1)
        attn_ref[s] = jnp.where(foreign_col, back, kept[s - 2]).astype(BF16)

    for copy in used:
        copy.wait_send()


def shards(
    geo,
    queries,
    new_kv,
    kv_pool,
    page_table,
    kv_lengths,
    slot_source,
    mamba_x,
    mamba_z,
    conv_state,
    ssm_state,
    x_proj_weight,
    dt_proj_weight,
    dt_bias,
    a_rate,
    skip_gain,
    conv_weight,
    conv_bias,
    dt_gain,
    b_gain,
    c_gain,
):
    nz, ny, nx = geo
    no = 2 * nx
    rpo = 64 // no
    copies = (
        (nz - 1) + 2 + (no - 1) + (ny - 1) + ny + 1 + 1 + (no - 1) + (no - 1) + 1 + 1
        + (nz - 1) + (ny - 1)
    )
    vmem = pl.BlockSpec(memory_space=pltpu.VMEM)
    scratch = [
        pltpu.VMEM(kv_pool.shape, BF16),
        pltpu.VMEM(ssm_state.shape, F32),
        pltpu.VMEM(x_proj_weight.shape, BF16),
        pltpu.VMEM(dt_proj_weight.shape, BF16),
        pltpu.VMEM((16, 16, 1024), F32),
        pltpu.VMEM((4, 16, 1024), F32),
        pltpu.VMEM((4, 16, 1024), F32),
        pltpu.VMEM((4, 16, 1024), F32),
        pltpu.VMEM((64, 512), F32),
        pltpu.VMEM((64, 128), F32),
        pltpu.VMEM((nz, 16, 512), BF16),
        pltpu.VMEM((ny, 16, 512), BF16),
        pltpu.VMEM((ny, 16, 512), BF16),
        pltpu.VMEM((ny, 16, 256), BF16),
        pltpu.VMEM((4, 16, 512), BF16),
        pltpu.VMEM((4, 16, 128), BF16),
        pltpu.VMEM((no, rpo, 640), F32),
        pltpu.VMEM((no, rpo, 640), F32),
        pltpu.VMEM((2 * rpo, 384), BF16),
        pltpu.VMEM((2 * rpo, 384), BF16),
        pltpu.VMEM((2 * rpo, 384), BF16),
        pltpu.VMEM((no, 2 * rpo, 384), BF16),
        pltpu.VMEM((256, 256), F32),
        pltpu.VMEM((256, 256), F32),
        pltpu.VMEM((256, 256), F32),
        pltpu.VMEM((16, 256), BF16),
        pltpu.VMEM((no, 16, 256), BF16),
        pltpu.VMEM((16, 256), BF16),
        pltpu.VMEM((16, 256), BF16),
        pltpu.VMEM((32, 256), F32),
        pltpu.VMEM((32, 256), F32),
        pltpu.VMEM((nz, 16, 384), BF16),
        pltpu.VMEM((ny, 16, 384), BF16),
        pltpu.VMEM((ny, 16, 384), BF16),
        pltpu.VMEM((16, 1024), F32),
        pltpu.VMEM((16, 1024), BF16),
        pltpu.SemaphoreType.DMA((copies,)),
        pltpu.SemaphoreType.DMA((copies,)),
        pltpu.SemaphoreType.DMA((4,)),
    ]
    return pl.pallas_call(
        functools.partial(kernel, geo),
        out_shape=(
            jax.ShapeDtypeStruct(queries.shape, BF16),
            jax.ShapeDtypeStruct(mamba_x.shape, BF16),
        ),
        in_specs=[pl.BlockSpec(memory_space=pltpu.SMEM)]
        + [vmem] * 16
        + [pl.BlockSpec(memory_space=pl.ANY)] * 4,
        out_specs=(vmem, vmem),
        scratch_shapes=scratch,
        compiler_params=pltpu.CompilerParams(
            collective_id=0, has_side_effects=True, vmem_limit_bytes=48 * 1024 * 1024
        ),
    )(
        slot_source,
        slot_source.reshape(1, -1),
        kv_lengths.reshape(1, -1),
        page_table,
        queries,
        new_kv,
        mamba_x,
        mamba_z,
        conv_state,
        dt_bias.reshape(1, -1),
        a_rate,
        skip_gain.reshape(1, -1),
        conv_weight,
        conv_bias.reshape(1, -1),
        dt_gain.reshape(1, -1),
        b_gain.reshape(1, -1),
        c_gain.reshape(1, -1),
        kv_pool,
        ssm_state,
        x_proj_weight,
        dt_proj_weight,
    )


def solution(mesh):
    placed = (
        P(None, "rep", "tp"),
        P(None, "rep", "tp"),
        P("rep", "tp", None, None),
        P("rep", None),
        P(),
        P(),
        P(None, "rep", "tp"),
        P(None, "rep", "tp"),
        P("rep", None, "tp"),
        P("rep", None, "tp"),
        P(None, "tp"),
        P(None, "tp"),
        P("tp"),
        P(None, "tp"),
        P("tp"),
        P(None, "tp"),
        P("tp"),
        P(),
        P(),
        P(),
    )
    return jax.shard_map(
        functools.partial(shards, geometry(mesh)),
        mesh=mesh,
        in_specs=placed,
        out_specs=(P(None, "rep", "tp"), P(None, "rep", "tp")),
        check_vma=False,
    )
```

time: 766 us -> 72.2 us (0.09)
  the two profiles are of different devices: /device:TPU:8 before, /device:TPU:4 now
where the time goes in v1:
time: 72.2 us; the launch traced here: 71.4 us
  Pallas kernels  52.7 us (73%)
  local copies, waits for them, and re-layouts  18.1 us (25%)
    pallas_call x1, Pallas kernels, shards(): pl.pallas_call(functools.partial(kernel, geo), out_shape=(jax.ShapeDtypeS...  52.7 us
    unnamed x40, local copies, waits for them, and re-layouts  18.1 us

profile of v1, /device:TPU:4, one launch (start us, length us, event | category | flops | bytes accessed | tf_op | source)
XLA Modules:
  0.0 71.4 jit_solution(3525340445347619681)
XLA Ops:
  0.6 0.8 %copy.22.page_ref = s32[16,8]{1,0:T(8,128)S(1)} copy(s32[16,8]{0,1:T(8,128)} %param.23) | data formatting | bytes 1024 | tf_op args[3]
  1.4 1.0 %copy.23.conv_ref = bf16[16,3,1024]{2,1,0:T(4,128)(2,1)S(1)} copy(bf16[16,3,1024]{2,0,1:T(8,128)(2,1)} %param.28) | data formatting | bytes 196608 | tf_op args[8]
  2.4 0.0 copy-start
  2.4 1.2 %copy-done = bf16[544,1024]{1,0:T(8,128)(2,1)S(1)} copy-done((bf16[544,1024]{1,0:T(8,128)(2,1)S(1)}, bf16[544,1024]{1,0:T(8,128)(2,1)}, u32[]{:S(2)}) %copy-start) | copy-done | bytes 1114136
  3.6 0.0 copy-start.1
  3.6 1.2 %copy-done.1 = f32[16,16,1024]{2,1,0:T(8,128)S(1)} copy-done((f32[16,16,1024]{2,1,0:T(8,128)S(1)}, f32[16,16,1024]{2,1,0:T(8,128)}, u32[]{:S(2)}) %copy-start.1) | copy-done | bytes 1048600
  4.8 0.0 copy-start.2
  4.8 1.2 %copy-done.2 = bf16[512,1024]{1,0:T(8,128)(2,1)S(1)} copy-done((bf16[512,1024]{1,0:T(8,128)(2,1)S(1)}, bf16[512,1024]{1,0:T(8,128)(2,1)}, u32[]{:S(2)}) %copy-start.2) | copy-done | bytes 1048600
  6.1 0.0 copy-start.3
  6.1 1.0 %copy-done.3 = bf16[64,1,16,256]{3,2,1,0:T(8,128)(2,1)S(1)} copy-done((bf16[64,1,16,256]{3,2,1,0:T(8,128)(2,1)S(1)}, bf16[64,1,16,256]{3,2,1,0:T(8,128)(2,1)}, u32[]{:S(2)}) %copy-start.3) | copy-done | bytes 524312
  7.1 0.0 copy-start.4
  7.1 0.9 %copy-done.4 = bf16[4,16,1024]{2,1,0:T(8,128)(2,1)S(1)} copy-done((bf16[4,16,1024]{2,1,0:T(8,128)(2,1)S(1)}, bf16[4,16,1024]{2,1,0:T(8,128)(2,1)}, u32[]{:S(2)}) %copy-start.4) | copy-done | bytes 131096
  8.0 0.0 copy-start.5
  8.0 0.9 %copy-done.5 = bf16[4,16,1024]{2,1,0:T(8,128)(2,1)S(1)} copy-done((bf16[4,16,1024]{2,1,0:T(8,128)(2,1)S(1)}, bf16[4,16,1024]{2,1,0:T(8,128)(2,1)}, u32[]{:S(2)}) %copy-start.5) | copy-done | bytes 131096
  8.9 0.0 copy-start.6
  8.9 0.8 %copy-done.6 = bf16[4,16,512]{2,1,0:T(8,128)(2,1)S(1)} copy-done((bf16[4,16,512]{2,1,0:T(8,128)(2,1)S(1)}, bf16[4,16,512]{2,1,0:T(8,128)(2,1)}, u32[]{:S(2)}) %copy-start.6) | copy-done | bytes 65560
  9.8 0.0 copy-start.7
  9.8 0.8 %copy-done.7 = f32[16,1024]{1,0:T(8,128)S(1)} copy-done((f32[16,1024]{1,0:T(8,128)S(1)}, f32[16,1024]{1,0:T(8,128)}, u32[]{:S(2)}) %copy-start.7) | copy-done | bytes 65560
  10.6 0.0 copy-start.8
  10.6 0.7 %copy-done.8 = bf16[4,16,128]{2,1,0:T(8,128)(2,1)S(1)} copy-done((bf16[4,16,128]{2,1,0:T(8,128)(2,1)S(1)}, bf16[4,16,128]{2,1,0:T(8,128)(2,1)}, u32[]{:S(2)}) %copy-start.8) | copy-done | bytes 16408
  11.3 0.0 copy-start.9
  11.3 0.7 %copy-done.9 = f32[4,1024]{1,0:T(4,128)S(1)} copy-done((f32[4,1024]{1,0:T(4,128)S(1)}, f32[4,1024]{1,0:T(4,128)}, u32[]{:S(2)}) %copy-start.9) | copy-done | bytes 16408
  12.0 0.0 copy-start.10
  12.0 0.7 copy-done.10
  12.7 0.0 copy-start.11
  12.7 0.7 copy-done.11
  13.4 0.0 copy-start.12
  13.4 0.7 copy-done.12
  14.1 0.0 copy-start.13
  14.1 0.7 copy-done.13
  14.8 0.0 copy-start.14
  14.8 0.7 copy-done.14
  15.5 0.0 copy-start.15
  15.5 0.7 copy-done.15
  16.1 0.0 copy-start.16
  16.1 0.7 copy-done.16
  16.8 0.0 copy-start.17
  16.8 0.7 copy-done.17
  17.5 52.7 %shard_map.203 = (bf16[4,16,512]{2,1,0:T(8,128)(2,1)S(1)}, bf16[4,16,1024]{2,1,0:T(8,128)(2,1)S(1)}) custom-call(s32[512]{0:T(512)S(1)} %copy-done.10, s32[1,512]{1,0:T(1,128)S(1)} %bitcast.8, s32[1,512]{1,0:T(1,128)S(1)} %bitcast.12, s32[16,8]{1,0:T(8,128)S(1)} %copy.22.page_ref, bf16[4,16,512]{2,1,0:T(8,128)(2,1)S(1)} %copy-done.6, ...), custom_call_target="tpu_custom_call" | custom-call | tf_op jit(solution)/shard_map/pallas_call | solution.py:665
  70.1 0.6 copy.26
  70.8 0.7 copy.27
Async XLA Ops:
  2.4 1.3 %copy-start = (bf16[544,1024]{1,0:T(8,128)(2,1)S(1)}, bf16[544,1024]{1,0:T(8,128)(2,1)}, u32[]{:S(2)}) copy-start(bf16[544,1024]{1,0:T(8,128)(2,1)} %xw_hbm.1) | copy-start | bytes 3342340
  3.6 1.2 %copy-start.1 = (f32[16,16,1024]{2,1,0:T(8,128)S(1)}, f32[16,16,1024]{2,1,0:T(8,128)}, u32[]{:S(2)}) copy-start(f32[16,16,1024]{2,1,0:T(8,128)} %ssm_hbm.1) | copy-start | bytes 3145732
  4.8 1.2 %copy-start.2 = (bf16[512,1024]{1,0:T(8,128)(2,1)S(1)}, bf16[512,1024]{1,0:T(8,128)(2,1)}, u32[]{:S(2)}) copy-start(bf16[512,1024]{1,0:T(8,128)(2,1)} %dw_hbm.1) | copy-start | bytes 3145732
  6.1 1.0 %copy-start.3 = (bf16[64,1,16,256]{3,2,1,0:T(8,128)(2,1)S(1)}, bf16[64,1,16,256]{3,2,1,0:T(8,128)(2,1)}, u32[]{:S(2)}) copy-start(bf16[64,1,16,256]{3,2,1,0:T(8,128)(2,1)} %pool_hbm.1) | copy-start | bytes 1572868
  7.1 0.9 %copy-start.4 = (bf16[4,16,1024]{2,1,0:T(8,128)(2,1)S(1)}, bf16[4,16,1024]{2,1,0:T(8,128)(2,1)}, u32[]{:S(2)}) copy-start(bf16[4,16,1024]{2,1,0:T(8,128)(2,1)} %x_ref.1) | copy-start | bytes 393220
  8.0 0.9 %copy-start.5 = (bf16[4,16,1024]{2,1,0:T(8,128)(2,1)S(1)}, bf16[4,16,1024]{2,1,0:T(8,128)(2,1)}, u32[]{:S(2)}) copy-start(bf16[4,16,1024]{2,1,0:T(8,128)(2,1)} %z_ref.1) | copy-start | bytes 393220
  8.9 0.8 %copy-start.6 = (bf16[4,16,512]{2,1,0:T(8,128)(2,1)S(1)}, bf16[4,16,512]{2,1,0:T(8,128)(2,1)}, u32[]{:S(2)}) copy-start(bf16[4,16,512]{2,1,0:T(8,128)(2,1)} %q_ref.1) | copy-start | bytes 196612
  9.8 0.8 %copy-start.7 = (f32[16,1024]{1,0:T(8,128)S(1)}, f32[16,1024]{1,0:T(8,128)}, u32[]{:S(2)}) copy-start(f32[16,1024]{1,0:T(8,128)} %a_ref.1) | copy-start | bytes 196612
  10.6 0.7 %copy-start.8 = (bf16[4,16,128]{2,1,0:T(8,128)(2,1)S(1)}, bf16[4,16,128]{2,1,0:T(8,128)(2,1)}, u32[]{:S(2)}) copy-start(bf16[4,16,128]{2,1,0:T(8,128)(2,1)} %nk_ref.1) | copy-start | bytes 49156
  11.3 0.7 %copy-start.9 = (f32[4,1024]{1,0:T(4,128)S(1)}, f32[4,1024]{1,0:T(4,128)}, u32[]{:S(2)}) copy-start(f32[4,1024]{1,0:T(4,128)} %cw_ref.1) | copy-start | bytes 49156
  12.0 0.7 copy-start.10
  12.7 0.7 copy-start.11
  13.4 0.7 copy-start.12
  14.1 0.7 copy-start.13
  14.8 0.7 copy-start.14
  15.5 0.7 copy-start.15
  16.1 0.7 copy-start.16
  16.8 0.7 copy-start.17

commit v2 on v1

--- a/solution.py
+++ b/solution.py
@@ -91,33 +91,50 @@
 
 def kernel(
     geo,
-    src_s,
+    src_ref_h,
+    q_ref_h,
+    nk_ref_h,
+    x_ref_h,
+    src_s_h,
+    conv_ref_h,
+    cw_ref_h,
+    cb_ref_h,
+    xw_h,
+    page_ref_h,
+    len_ref_h,
+    pool_h,
+    dtg_ref_h,
+    dw_h,
+    dtb_ref_h,
+    bg_ref_h,
+    cg_ref_h,
+    skip_ref_h,
+    a_ref_h,
+    ssm_h,
+    z_ref_h,
+    attn_ref,
+    mix_ref,
     src_ref,
-    len_ref,
-    page_ref,
     q_ref,
     nk_ref,
     x_ref,
-    z_ref,
+    src_s,
     conv_ref,
-    dtb_ref,
-    a_ref,
-    skip_ref,
     cw_ref,
     cb_ref,
+    xw,
+    page_ref,
+    len_ref,
+    pool,
     dtg_ref,
+    dw,
+    dtb_ref,
     bg_ref,
     cg_ref,
-    pool_hbm,
-    ssm_hbm,
-    xw_hbm,
-    dw_hbm,
-    attn_ref,
-    mix_ref,
-    pool,
+    skip_ref,
+    a_ref,
     ssm,
-    xw,
-    dw,
+    z_ref,
     mid,
     act,
     dts,
@@ -186,11 +203,38 @@
             barrier, inc=1, device_id=device, device_id_type=pl.DeviceIdType.MESH
         )
 
-    loads = []
-    for k, (a, b) in enumerate(((xw_hbm, xw), (pool_hbm, pool), (dw_hbm, dw), (ssm_hbm, ssm))):
-        load = pltpu.make_async_copy(a, b, lsem.at[k])
-        load.start()
-        loads.append(load)
+    loads = {}
+    for k, (name, a, b) in enumerate(
+        (
+            ("src_ref", src_ref_h, src_ref),
+            ("q_ref", q_ref_h, q_ref),
+            ("nk_ref", nk_ref_h, nk_ref),
+            ("x_ref", x_ref_h, x_ref),
+            ("src_s", src_s_h, src_s),
+            ("conv_ref", conv_ref_h, conv_ref),
+            ("cw_ref", cw_ref_h, cw_ref),
+            ("cb_ref", cb_ref_h, cb_ref),
+            ("xw", xw_h, xw),
+            ("page_ref", page_ref_h, page_ref),
+            ("len_ref", len_ref_h, len_ref),
+            ("pool", pool_h, pool),
+            ("dtg_ref", dtg_ref_h, dtg_ref),
+            ("dw", dw_h, dw),
+            ("dtb_ref", dtb_ref_h, dtb_ref),
+            ("bg_ref", bg_ref_h, bg_ref),
+            ("cg_ref", cg_ref_h, cg_ref),
+            ("skip_ref", skip_ref_h, skip_ref),
+            ("a_ref", a_ref_h, a_ref),
+            ("ssm", ssm_h, ssm),
+            ("z_ref", z_ref_h, z_ref),
+        )
+    ):
+        loads[name] = pltpu.make_async_copy(a, b, lsem.at[k])
+        loads[name].start()
+
+    def need(*names):
+        for name in names:
+            loads[name].wait()
 
     used = []
 
@@ -208,6 +252,7 @@
         used.append(copy)
         return copy
 
+    need("src_ref")
     src = src_ref[...]
     lane_n = iota((1, n), 1)
     foreign = src != lane_n
@@ -225,6 +270,7 @@
     pack = hot(place & ((row >> 2) == ((col >> 4) & 3)) & ((row & 1) == (col >> 6)))
     pick16 = hot(place & (col < 16))[:, :16]
 
+    need("q_ref", "nk_ref", "x_ref")
     blocks = []
     nothing = jnp.zeros((16, 256), BF16)
     for s in (2, 3):
@@ -246,8 +292,8 @@
     q_swap = push(q_ref, q_other, (rep, tp_other))
     nk_swap = push(nk_ref, nk_other, (rep, tp_other))
 
-    conv = conv_ref[...].astype(F32)
-    window = [conv[:, w, :] for w in range(3)] + [x_ref[s].astype(F32) for s in range(4)]
+    need("conv_ref", "cw_ref", "cb_ref")
+    window = [conv_ref[w].astype(F32) for w in range(3)] + [x_ref[s].astype(F32) for s in range(4)]
     conv_last = window[2].astype(BF16)
     cw = cw_ref[...]
     cb = cb_ref[...]
@@ -259,7 +305,7 @@
         activ.append(silu(total + cb))
         act[s] = activ[s]
     activ_b = jnp.concatenate([v.astype(BF16) for v in activ], axis=0)
-    loads[0].wait()
+    need("xw")
 
     def project(rows):
         tail = jnp.concatenate([xw[512:544, :], jnp.zeros((96, 1024), BF16)], axis=0)
@@ -289,16 +335,19 @@
     select_in = hot(alike & (nt(hot(donor == to_code), hot(home == from_code)) > 0.5))
     select_out = hot(alike & (nt(hot(home == to_code), hot(donor == from_code)) > 0.5))
 
+    need("page_ref", "len_ref")
     own_lane = iota((16, n), 1) == rep * 16 + iota((16, n), 0)
     lengths = jnp.sum(jnp.where(own_lane, len_ref[...], 0), axis=1, keepdims=True)
     foreign_col = (
         jnp.sum(jnp.where(own_lane & foreign, 1.0, 0.0), axis=1, keepdims=True) > 0.5
     )
     table = page_ref[...]
+    eye = iota((16, 16), 0) == iota((16, 16), 1)
     cache_lane = iota((16, 1024), 1)
     allowed = jnp.zeros((16, 1024), F32)
     for k in range(4):
-        page = jnp.where(core == 0, table[:, 2 * k : 2 * k + 1], table[:, 2 * k + 1 : 2 * k + 2])
+        page = jnp.where(core == 0, table[2 * k : 2 * k + 1], table[2 * k + 1 : 2 * k + 2])
+        page = jnp.sum(jnp.where(eye, page, 0), axis=1, keepdims=True)
         limit = lengths - (2 * k + core) * 16
         allowed = jnp.where(
             ((cache_lane >> 4) == page) & ((cache_lane & 15) < limit), 1.0, allowed
@@ -340,7 +389,7 @@
     half_send[...] = pack_half(summed)
     half = push(half_send, half_land, (rep, tp_half))
 
-    loads[1].wait()
+    need("pool")
     q_swap.wait_recv()
     nk_swap.wait_recv()
     pages = pool[...].reshape(1024, 256)
@@ -399,6 +448,7 @@
     late_send[...] = late_own.astype(BF16)
     late_out = [push(late_send, late_land.at[d], (rep, o_tp(d))) for d in range(1, no)]
 
+    need("dtg_ref")
     half.wait_recv()
     summed = summed + unpack_half(half_land[...])
     main = summed[:, 0:512]
@@ -464,15 +514,13 @@
     for d, copy in enumerate(norm_out, 1):
         copy.wait_recv()
         take((own - d + no) % no, norm_land[d])
-    loads[2].wait()
+    need("dw", "dtb_ref", "bg_ref", "cg_ref", "skip_ref", "a_ref", "ssm")
     steps = softplus(nn(dtl[...].astype(BF16), dw[...]) + dtb_ref[...])
     for s in range(4):
         dts[s] = steps[s * 16 : (s + 1) * 16]
-    eye = iota((16, 16), 0) == iota((16, 16), 1)
     b_gain = jnp.sum(jnp.where(eye, bg_ref[...], 0.0), axis=1, keepdims=True)
     c_gain = jnp.sum(jnp.where(eye, cg_ref[...], 0.0), axis=1, keepdims=True)
     skip = skip_ref[...]
-    loads[3].wait()
 
     def columns(tail_row):
         b = jnp.sum(jnp.where(col == row, tail_row, 0.0), axis=1, keepdims=True) * b_gain
@@ -521,6 +569,7 @@
     late_dt = softplus(nn(low.astype(BF16), dw[...]) + dtb_ref[...])
     late_tail = tail_norm(late_sum[:, 128:256])
 
+    need("src_s")
     base = rep * 16
     first = jnp.int32(-1)
     second = jnp.int32(0)
@@ -549,6 +598,7 @@
     z_out = [push(gather_out.at[0], gather_out.at[d], (z_rep(d), tp)) for d in range(1, nz)]
 
     scan(2, mid, False)
+    need("z_ref")
     partial.wait_recv()
     kept = []
     for s in range(4):
@@ -620,12 +670,34 @@
         (nz - 1) + 2 + (no - 1) + (ny - 1) + ny + 1 + 1 + (no - 1) + (no - 1) + 1 + 1
         + (nz - 1) + (ny - 1)
     )
+    operands = (
+        slot_source.reshape(1, -1),
+        queries,
+        new_kv,
+        mamba_x,
+        slot_source,
+        conv_state.transpose(1, 0, 2),
+        conv_weight,
+        conv_bias.reshape(1, -1),
+        x_proj_weight,
+        page_table.T,
+        kv_lengths.reshape(1, -1),
+        kv_pool,
+        dt_gain.reshape(1, -1),
+        dt_proj_weight,
+        dt_bias.reshape(1, -1),
+        b_gain.reshape(1, -1),
+        c_gain.reshape(1, -1),
+        skip_gain.reshape(1, -1),
+        a_rate,
+        ssm_state,
+        mamba_z,
+    )
     vmem = pl.BlockSpec(memory_space=pltpu.VMEM)
     scratch = [
-        pltpu.VMEM(kv_pool.shape, BF16),
-        pltpu.VMEM(ssm_state.shape, F32),
-        pltpu.VMEM(x_proj_weight.shape, BF16),
-        pltpu.VMEM(dt_proj_weight.shape, BF16),
+        pltpu.SMEM(v.shape, v.dtype) if k == 4 else pltpu.VMEM(v.shape, v.dtype)
+        for k, v in enumerate(operands)
+    ] + [
         pltpu.VMEM((16, 16, 1024), F32),
         pltpu.VMEM((4, 16, 1024), F32),
         pltpu.VMEM((4, 16, 1024), F32),
@@ -660,7 +732,7 @@
         pltpu.VMEM((16, 1024), BF16),
         pltpu.SemaphoreType.DMA((copies,)),
         pltpu.SemaphoreType.DMA((copies,)),
-        pltpu.SemaphoreType.DMA((4,)),
+        pltpu.SemaphoreType.DMA((len(operands),)),
     ]
     return pl.pallas_call(
         functools.partial(kernel, geo),
@@ -668,37 +740,13 @@
             jax.ShapeDtypeStruct(queries.shape, BF16),
             jax.ShapeDtypeStruct(mamba_x.shape, BF16),
         ),
-        in_specs=[pl.BlockSpec(memory_space=pltpu.SMEM)]
-        + [vmem] * 16
-        + [pl.BlockSpec(memory_space=pl.ANY)] * 4,
+        in_specs=[pl.BlockSpec(memory_space=pl.ANY)] * len(operands),
         out_specs=(vmem, vmem),
         scratch_shapes=scratch,
         compiler_params=pltpu.CompilerParams(
-            collective_id=0, has_side_effects=True, vmem_limit_bytes=48 * 1024 * 1024
+            collective_id=0, has_side_effects=True, vmem_limit_bytes=60 * 1024 * 1024
         ),
-    )(
-        slot_source,
-        slot_source.reshape(1, -1),
-        kv_lengths.reshape(1, -1),
-        page_table,
-        queries,
-        new_kv,
-        mamba_x,
-        mamba_z,
-        conv_state,
-        dt_bias.reshape(1, -1),
-        a_rate,
-        skip_gain.reshape(1, -1),
-        conv_weight,
-        conv_bias.reshape(1, -1),
-        dt_gain.reshape(1, -1),
-        b_gain.reshape(1, -1),
-        c_gain.reshape(1, -1),
-        kv_pool,
-        ssm_state,
-        x_proj_weight,
-        dt_proj_weight,
-    )
+    )(*operands)
 
 
 def solution(mesh):

time: 72.2 us -> 56.9 us (0.79)
  local copies, waits for them, and re-layouts: 18.1 us -> 3.04 us
    unnamed x40 -> x2, local copies, waits for them, and re-layouts: 18.1 us -> 3.04 us
where the time goes in v2:
time: 56.9 us; the launch traced here: 56.7 us
  Pallas kernels  53 us (93%)
  local copies, waits for them, and re-layouts  3.04 us (5%)
  between operations  0.65 us (1%)
    pallas_call x1, Pallas kernels, shards(): pl.pallas_call(functools.partial(kernel, geo), out_shape=(jax.ShapeDtypeS...  53 us
    unnamed x2, local copies, waits for them, and re-layouts  3.04 us

profile of v2, /device:TPU:4, one launch (start us, length us, event | category | flops | bytes accessed | tf_op | source)
XLA Modules:
  0.0 56.7 jit_solution(17241066409925835910)
XLA Ops:
  0.6 53.0 %shard_map.203 = (bf16[4,16,512]{2,1,0:T(8,128)(2,1)}, bf16[4,16,1024]{2,1,0:T(8,128)(2,1)}) custom-call(s32[1,512]{1,0:T(1,128)} %bitcast.11, bf16[4,16,512]{2,1,0:T(8,128)(2,1)} %q_ref_h.1, bf16[4,16,128]{2,1,0:T(8,128)(2,1)} %nk_ref_h.1, bf16[4,16,1024]{2,1,0:T(8,128)(2,1)} %x_ref_h.1, s32[512]{0:T(512)} %src_s_h.1, bf16[3,16,1024]{2,1,0:T(8,128)(2,1)} %bitcast.10, ...), custom_call_target="tpu_custom_call" | custom-call | tf_op jit(solution)/shard_map/pallas_call | solution.py:737
  53.7 1.5 %copy.24 = bf16[4,16,512]{2,1,0:T(8,128)(2,1)} copy(bf16[4,16,512]{2,1,0:T(8,128)(2,1)} %get-tuple-element.4) | data formatting | bytes 131072
  55.1 1.6 %copy.25 = bf16[4,16,1024]{2,1,0:T(8,128)(2,1)} copy(bf16[4,16,1024]{2,1,0:T(8,128)(2,1)} %get-tuple-element.5) | data formatting | bytes 262144

commit v3 on v2

--- a/solution.py
+++ b/solution.py
@@ -141,9 +141,12 @@
     mixed,
     dtl,
     tails,
-    gather_in,
-    stage_y,
-    land_y,
+    gather_x,
+    stage_x,
+    land_x,
+    gather_q,
+    stage_q,
+    land_q,
     land_o,
     q_other,
     nk_other,
@@ -162,14 +165,18 @@
     late_half_land,
     late_away,
     late_far,
-    gather_out,
-    stage_r,
-    land_r,
+    gather_m,
+    stage_m,
+    land_m,
+    gather_a,
+    stage_a,
+    land_a,
     bias_ref,
     mask_ref,
     ssem,
     rsem,
     lsem,
+    ready,
 ):
     nz, ny, nx = geo
     no = 2 * nx
@@ -196,7 +203,8 @@
     partners += [(y_rep(e), tp) for e in range(1, ny)]
     partners += [(y_rep(e), tp_other) for e in range(1, ny)]
     partners += [(rep, o_tp(d)) for d in range(1, no)]
-    partners += [(rep, tp_half)]
+    mirror = ((nz - 1 - zi) * ny + yi, tp_half)
+    partners += [mirror]
     barrier = pltpu.get_barrier_semaphore()
     for device in partners:
         pl.semaphore_signal(
@@ -284,11 +292,15 @@
                 else (jnp.concatenate([nk_s, nothing[:, :128]], axis=1) if b == 2 else nothing)
             )
             blocks.append(jnp.concatenate([x_s[:, b * 256 : (b + 1) * 256], side], axis=1))
-    gather_in[0] = nn(pack, jnp.concatenate(blocks, axis=0)).astype(BF16)
+    item = nn(pack, jnp.concatenate(blocks, axis=0)).astype(BF16)
+    gather_x[0] = item[:, 0:256]
+    gather_q[0] = item[:, 256:512]
 
     pl.semaphore_wait(barrier, len(partners))
-
-    z_in = [push(gather_in.at[0], gather_in.at[d], (z_rep(d), tp)) for d in range(1, nz)]
+    pl.semaphore_signal(ready, inc=1, device_id=mirror, device_id_type=pl.DeviceIdType.MESH)
+
+    z_x = [push(gather_x.at[0], gather_x.at[d], (z_rep(d), tp)) for d in range(1, nz)]
+    z_q = [push(gather_q.at[0], gather_q.at[d], (z_rep(d), tp)) for d in range(1, nz)]
     q_swap = push(q_ref, q_other, (rep, tp_other))
     nk_swap = push(nk_ref, nk_other, (rep, tp_other))
 
@@ -335,6 +347,45 @@
     select_in = hot(alike & (nt(hot(donor == to_code), hot(home == from_code)) > 0.5))
     select_out = hot(alike & (nt(hot(home == to_code), hot(donor == from_code)) > 0.5))
 
+    def select(copies, chooser, gathered, staged, landing):
+        for copy in copies:
+            copy.wait_recv()
+        width = gathered.shape[2]
+        chosen = nn(chooser, gathered[...].reshape(nz * 16, width)).astype(BF16)
+        for e in range(ny):
+            staged[e] = chosen[e * 16 : (e + 1) * 16]
+        landing[0] = chosen[0:16]
+        return [push(staged.at[e], landing.at[e], (y_rep(e), tp)) for e in range(1, ny)]
+
+    y_x = select(z_x, select_in, gather_x, stage_x, land_x)
+
+    for copy in part_out:
+        copy.wait_recv()
+    summed = part[own]
+    for d in range(1, no):
+        summed = summed + part_land[d]
+    blank = jnp.zeros((rpo, 128), F32)
+
+    def pack_half(v):
+        return jnp.concatenate(
+            [
+                jnp.concatenate([v[:, 0:256], v[:, 512:640]], axis=1),
+                jnp.concatenate([v[:, 256:512], blank], axis=1),
+            ],
+            axis=0,
+        ).astype(BF16)
+
+    def unpack_half(v):
+        v = v.astype(F32)
+        return jnp.concatenate([v[:rpo, 0:256], v[rpo:, 0:256], v[:rpo, 256:384]], axis=1)
+
+    half_send[...] = pack_half(summed)
+    pl.semaphore_wait(ready, 1)
+    half = push(half_send, half_land, (rep, tp_half))
+
+    y_q = select(z_q, select_in, gather_q, stage_q, land_q)
+    y_q += [push(stage_q.at[e], land_o.at[e], (y_rep(e), tp_other)) for e in range(ny)]
+
     need("page_ref", "len_ref")
     own_lane = iota((16, n), 1) == rep * 16 + iota((16, n), 0)
     lengths = jnp.sum(jnp.where(own_lane, len_ref[...], 0), axis=1, keepdims=True)
@@ -355,39 +406,36 @@
     mask_ref[...] = allowed.astype(BF16)
     bias_ref[...] = jnp.where(allowed > 0.5, 0.0, MASKED)
 
-    for copy in z_in:
+    for copy in y_x:
         copy.wait_recv()
-    chosen = nn(select_in, gather_in[...].reshape(nz * 16, 512)).astype(BF16)
-    for e in range(ny):
-        stage_y[e] = chosen[e * 16 : (e + 1) * 16]
-    land_y[0] = chosen[0:16]
-    y_in = [push(stage_y.at[e], land_y.at[e], (y_rep(e), tp)) for e in range(1, ny)]
-    y_in += [
-        push(stage_y.at[e, :, 256:512], land_o.at[e], (y_rep(e), tp_other)) for e in range(ny)
-    ]
-
-    for copy in part_out:
-        copy.wait_recv()
-    summed = part[own]
-    for d in range(1, no):
-        summed = summed + part_land[d]
-    blank = jnp.zeros((rpo, 128), F32)
-
-    def pack_half(v):
-        return jnp.concatenate(
-            [
-                jnp.concatenate([v[:, 0:256], v[:, 512:640]], axis=1),
-                jnp.concatenate([v[:, 256:512], blank], axis=1),
-            ],
-            axis=0,
-        ).astype(BF16)
-
-    def unpack_half(v):
-        v = v.astype(F32)
-        return jnp.concatenate([v[:rpo, 0:256], v[rpo:, 0:256], v[:rpo, 256:384]], axis=1)
-
-    half_send[...] = pack_half(summed)
-    half = push(half_send, half_land, (rep, tp_half))
+    er = iota((128, ny * 16), 0)
+    ec = iota((128, ny * 16), 1)
+    wanted_step = jnp.where(er < 64, er & 1, 0)
+    expand = hot(
+        (((er >> 4) & 3) == ((ec >> 2) & 3))
+        & (((er >> 1) & 1) == ((ec >> 1) & 1))
+        & (wanted_step == (ec & 1))
+    )
+    arrived = nn(expand, land_x[...].reshape(ny * 16, 256))
+    x_now = jnp.concatenate([arrived[b * 16 : (b + 1) * 16] for b in range(4)], axis=1)
+    x_prev = jnp.concatenate(
+        [arrived[64 + b * 16 : 64 + (b + 1) * 16] for b in range(4)], axis=1
+    )
+    last_row = nn(pick16, conv_last)
+    x_zero = nn(pick16, x_ref[0])
+    x_one = nn(pick16, x_ref[1])
+    odd = (iota((16, 1024), 0) & 1) == 1
+    total = jnp.where(odd, x_zero, last_row) * cw[0:1]
+    total = total + jnp.where(odd, x_one, x_zero) * cw[1:2]
+    total = total + jnp.where(odd, x_prev, x_one) * cw[2:3]
+    total = total + x_now * cw[3:4]
+    late_act = silu(total + cb)
+    main, tail = project(late_act.astype(BF16))
+    late_own = jnp.concatenate(
+        [by_quarter([main[:, b * 128 : (b + 1) * 128] for b in range(4)]), tail], axis=1
+    )
+    late_send[...] = late_own.astype(BF16)
+    late_out = [push(late_send, late_land.at[d], (rep, o_tp(d))) for d in range(1, no)]
 
     need("pool")
     q_swap.wait_recv()
@@ -416,38 +464,6 @@
         if target is away:
             partial = push(away, far, (rep, tp_other))
 
-    for copy in y_in:
-        copy.wait_recv()
-    er = iota((128, ny * 16), 0)
-    ec = iota((128, ny * 16), 1)
-    wanted_step = jnp.where(er < 64, er & 1, 0)
-    expand = hot(
-        (((er >> 4) & 3) == ((ec >> 2) & 3))
-        & (((er >> 1) & 1) == ((ec >> 1) & 1))
-        & (wanted_step == (ec & 1))
-    )
-    arrived = nn(expand, land_y[...].reshape(ny * 16, 512))
-    arrived_o = nn(expand[0:64], land_o[...].reshape(ny * 16, 256))
-    x_now = jnp.concatenate([arrived[b * 16 : (b + 1) * 16, 0:256] for b in range(4)], axis=1)
-    x_prev = jnp.concatenate(
-        [arrived[64 + b * 16 : 64 + (b + 1) * 16, 0:256] for b in range(4)], axis=1
-    )
-    last_row = nn(pick16, conv_last)
-    x_zero = nn(pick16, x_ref[0])
-    x_one = nn(pick16, x_ref[1])
-    odd = (iota((16, 1024), 0) & 1) == 1
-    total = jnp.where(odd, x_zero, last_row) * cw[0:1]
-    total = total + jnp.where(odd, x_one, x_zero) * cw[1:2]
-    total = total + jnp.where(odd, x_prev, x_one) * cw[2:3]
-    total = total + x_now * cw[3:4]
-    late_act = silu(total + cb)
-    main, tail = project(late_act.astype(BF16))
-    late_own = jnp.concatenate(
-        [by_quarter([main[:, b * 128 : (b + 1) * 128] for b in range(4)]), tail], axis=1
-    )
-    late_send[...] = late_own.astype(BF16)
-    late_out = [push(late_send, late_land.at[d], (rep, o_tp(d))) for d in range(1, no)]
-
     need("dtg_ref")
     half.wait_recv()
     summed = summed + unpack_half(half_land[...])
@@ -467,17 +483,29 @@
 
     take(own, packed)
 
+    for copy in late_out:
+        copy.wait_recv()
+    late_sum = late_own
+    for d in range(1, no):
+        late_sum = late_sum + late_land[d].astype(F32)
+    late_half[...] = late_sum.astype(BF16)
+    late_swap = push(late_half, late_half_land, (rep, tp_half))
+
+    for copy in y_q:
+        copy.wait_recv()
+    arrived_q = nn(expand[0:64], land_q[...].reshape(ny * 16, 256))
+    arrived_o = nn(expand[0:64], land_o[...].reshape(ny * 16, 256))
     q_late = jnp.concatenate(
         [
-            v[(h // 2) * 16 : (h // 2) * 16 + 8, off + (h % 2) * 128 : off + (h % 2) * 128 + 128]
-            for v, off in ((arrived, 256), (arrived_o, 0))
+            v[(h // 2) * 16 : (h // 2) * 16 + 8, (h % 2) * 128 : (h % 2) * 128 + 128]
+            for v in (arrived_q, arrived_o)
             for h in range(4)
         ],
         axis=0,
     ).astype(BF16)
     pad48 = jnp.zeros((48, 128), BF16)
     late_keys = jnp.concatenate(
-        new_keys + [arrived[32:48, 256:384].astype(BF16), pad48], axis=0
+        new_keys + [arrived_q[32:48, 0:128].astype(BF16), pad48], axis=0
     )
     late_values = jnp.concatenate(
         new_values + [arrived_o[32:48, 0:128].astype(BF16), pad48], axis=0
@@ -502,14 +530,6 @@
     late_near = jnp.concatenate([out[0:32], stats[0:32]], axis=1)
     late_away[...] = jnp.concatenate([out[32:64], stats[32:64]], axis=1)
     late_partial = push(late_away, late_far, (rep, tp_other))
-
-    for copy in late_out:
-        copy.wait_recv()
-    late_sum = late_own
-    for d in range(1, no):
-        late_sum = late_sum + late_land[d].astype(F32)
-    late_half[...] = late_sum.astype(BF16)
-    late_swap = push(late_half, late_half_land, (rep, tp_half))
 
     for d, copy in enumerate(norm_out, 1):
         copy.wait_recv()
@@ -550,6 +570,14 @@
         lax.fori_loop(0, 16, body, 0)
 
     scan(0, ssm, True)
+
+    late_partial.wait_recv()
+    heads = combine(late_near, late_far[...]).astype(BF16)
+    hr = iota((16, 32), 0)
+    hc = iota((16, 32), 1)
+    heads = nn(hot(((hr >> 2) == (hc >> 3)) & ((hr & 3) == (hc & 7))), heads)
+    gather_a[0] = heads.astype(BF16)
+    z_a = [push(gather_a.at[0], gather_a.at[d], (z_rep(d), tp)) for d in range(1, nz)]
 
     late_swap.wait_recv()
     late_sum = late_sum + late_half_land[...].astype(F32)
@@ -588,14 +616,10 @@
                 state, late_dt[m : m + 1], late_act[m : m + 1], late_tail[m : m + 1]
             )
             late_mixed = jnp.where(rows == m, out, late_mixed)
-    late_partial.wait_recv()
-    heads = combine(late_near, late_far[...]).astype(BF16)
-    hr = iota((16, 32), 0)
-    hc = iota((16, 32), 1)
-    heads = nn(hot(((hr >> 2) == (hc >> 3)) & ((hr & 3) == (hc & 7))), heads)
-    quarter = by_quarter([late_mixed[:, b * 256 : (b + 1) * 256] for b in range(4)])
-    gather_out[0] = jnp.concatenate([quarter, heads], axis=1).astype(BF16)
-    z_out = [push(gather_out.at[0], gather_out.at[d], (z_rep(d), tp)) for d in range(1, nz)]
+    gather_m[0] = by_quarter(
+        [late_mixed[:, b * 256 : (b + 1) * 256] for b in range(4)]
+    ).astype(BF16)
+    z_m = [push(gather_m.at[0], gather_m.at[d], (z_rep(d), tp)) for d in range(1, nz)]
 
     scan(2, mid, False)
     need("z_ref")
@@ -610,13 +634,7 @@
         else:
             kept.append(block)
 
-    for copy in z_out:
-        copy.wait_recv()
-    chosen = nn(select_out, gather_out[...].reshape(nz * 16, 384)).astype(BF16)
-    for e in range(ny):
-        stage_r[e] = chosen[e * 16 : (e + 1) * 16]
-    land_r[0] = chosen[0:16]
-    y_out = [push(stage_r.at[e], land_r.at[e], (y_rep(e), tp)) for e in range(1, ny)]
+    y_a = select(z_a, select_out, gather_a, stage_a, land_a)
     own_code = rep * 2 + ((iota((ny * 16, n), 0) >> 1) & 1)
     fr = iota((128, ny * 16), 0)
     fc = iota((128, ny * 16), 1)
@@ -625,15 +643,17 @@
         & ((fr >> 6) == (fc & 1))
         & (nt(slot_pick, hot(home == own_code)) > 0.5)
     )
-    for copy in y_out:
+    y_m = select(z_m, select_out, gather_m, stage_m, land_m)
+    for copy in y_a + y_m:
         copy.wait_recv()
-    returned = nn(put, land_r[...].reshape(ny * 16, 384))
+    returned = nn(put, land_m[...].reshape(ny * 16, 256))
+    attended = nn(put, land_a[...].reshape(ny * 16, 128))
     for s in (2, 3):
-        pieces = [returned[(s - 2) * 64 + b * 16 : (s - 2) * 64 + b * 16 + 16] for b in range(4)]
-        back = jnp.concatenate([v[:, 0:256] for v in pieces], axis=1)
+        spots = [(s - 2) * 64 + b * 16 for b in range(4)]
+        back = jnp.concatenate([returned[p : p + 16] for p in spots], axis=1)
         whole = jnp.where(foreign_col, back, mixed[s])
         mix_ref[s] = (whole * silu(z_ref[s].astype(F32))).astype(BF16)
-        back = jnp.concatenate([v[:, 256:384] for v in pieces], axis=1)
+        back = jnp.concatenate([attended[p : p + 16] for p in spots], axis=1)
         attn_ref[s] = jnp.where(foreign_col, back, kept[s - 2]).astype(BF16)
 
     for copy in used:
@@ -666,10 +686,7 @@
     nz, ny, nx = geo
     no = 2 * nx
     rpo = 64 // no
-    copies = (
-        (nz - 1) + 2 + (no - 1) + (ny - 1) + ny + 1 + 1 + (no - 1) + (no - 1) + 1 + 1
-        + (nz - 1) + (ny - 1)
-    )
+    copies = 4 * (nz - 1) + 4 * (ny - 1) + ny + 3 * (no - 1) + 6
     operands = (
         slot_source.reshape(1, -1),
         queries,
@@ -704,9 +721,12 @@
         pltpu.VMEM((4, 16, 1024), F32),
         pltpu.VMEM((64, 512), F32),
         pltpu.VMEM((64, 128), F32),
-        pltpu.VMEM((nz, 16, 512), BF16),
-        pltpu.VMEM((ny, 16, 512), BF16),
-        pltpu.VMEM((ny, 16, 512), BF16),
+        pltpu.VMEM((nz, 16, 256), BF16),
+        pltpu.VMEM((ny, 16, 256), BF16),
+        pltpu.VMEM((ny, 16, 256), BF16),
+        pltpu.VMEM((nz, 16, 256), BF16),
+        pltpu.VMEM((ny, 16, 256), BF16),
+        pltpu.VMEM((ny, 16, 256), BF16),
         pltpu.VMEM((ny, 16, 256), BF16),
         pltpu.VMEM((4, 16, 512), BF16),
         pltpu.VMEM((4, 16, 128), BF16),
@@ -725,20 +745,24 @@
         pltpu.VMEM((16, 256), BF16),
         pltpu.VMEM((32, 256), F32),
         pltpu.VMEM((32, 256), F32),
-        pltpu.VMEM((nz, 16, 384), BF16),
-        pltpu.VMEM((ny, 16, 384), BF16),
-        pltpu.VMEM((ny, 16, 384), BF16),
+        pltpu.VMEM((nz, 16, 256), BF16),
+        pltpu.VMEM((ny, 16, 256), BF16),
+        pltpu.VMEM((ny, 16, 256), BF16),
+        pltpu.VMEM((nz, 16, 128), BF16),
+        pltpu.VMEM((ny, 16, 128), BF16),
+        pltpu.VMEM((ny, 16, 128), BF16),
         pltpu.VMEM((16, 1024), F32),
         pltpu.VMEM((16, 1024), BF16),
         pltpu.SemaphoreType.DMA((copies,)),
         pltpu.SemaphoreType.DMA((copies,)),
         pltpu.SemaphoreType.DMA((len(operands),)),
+        pltpu.SemaphoreType.REGULAR,
     ]
     return pl.pallas_call(
         functools.partial(kernel, geo),
         out_shape=(
-            jax.ShapeDtypeStruct(queries.shape, BF16),
-            jax.ShapeDtypeStruct(mamba_x.shape, BF16),
+            pltpu.VMEM(queries.shape, BF16),
+            pltpu.VMEM(mamba_x.shape, BF16),
         ),
         in_specs=[pl.BlockSpec(memory_space=pl.ANY)] * len(operands),
         out_specs=(vmem, vmem),

time: 56.9 us -> 51.2 us (0.90)
  the two profiles are of different devices: /device:TPU:4 before, /device:TPU:1 now
where the time goes in v3:
time: 51.2 us; the launch traced here: 50.5 us
  Pallas kernels  48.6 us (95%)
  local copies, waits for them, and re-layouts  1.29 us (3%)
  between operations  0.65 us (1%)
    pallas_call x1, Pallas kernels, shards(): pl.pallas_call(functools.partial(kernel, geo), out_shape=(pltpu.VMEM(quer...  48.6 us
    unnamed x2, local copies, waits for them, and re-layouts  1.29 us

profile of v3, /device:TPU:1, one launch (start us, length us, event | category | flops | bytes accessed | tf_op | source)
XLA Modules:
  0.0 50.5 jit_solution(7432921799491075625)
XLA Ops:
  0.6 48.6 %shard_map.203 = (bf16[4,16,512]{2,1,0:T(8,128)(2,1)S(1)}, bf16[4,16,1024]{2,1,0:T(8,128)(2,1)S(1)}) custom-call(s32[1,512]{1,0:T(1,128)} %bitcast.11, bf16[4,16,512]{2,1,0:T(8,128)(2,1)} %q_ref_h.1, bf16[4,16,128]{2,1,0:T(8,128)(2,1)} %nk_ref_h.1, bf16[4,16,1024]{2,1,0:T(8,128)(2,1)} %x_ref_h.1, s32[512]{0:T(512)} %src_s_h.1, ...), custom_call_target="tpu_custom_call" | custom-call | tf_op jit(solution)/shard_map/pallas_call | solution.py:761
  49.3 0.6 %copy.24 = bf16[4,16,512]{2,1,0:T(8,128)(2,1)} copy(bf16[4,16,512]{2,1,0:T(8,128)(2,1)S(1)} %get-tuple-element.2) | data formatting | bytes 131072
  49.9 0.7 %copy.25 = bf16[4,16,1024]{2,1,0:T(8,128)(2,1)} copy(bf16[4,16,1024]{2,1,0:T(8,128)(2,1)S(1)} %get-tuple-element.3) | data formatting | bytes 262144

commit v4 on v3

--- a/solution.py
+++ b/solution.py
@@ -141,6 +141,7 @@
     mixed,
     dtl,
     tails,
+    item_x,
     gather_x,
     stage_x,
     land_x,
@@ -163,8 +164,11 @@
     late_land,
     late_half,
     late_half_land,
+    late_acc,
+    late_total,
     late_away,
     late_far,
+    item_m,
     gather_m,
     stage_m,
     land_m,
@@ -177,6 +181,14 @@
     rsem,
     lsem,
     ready,
+    zs,
+    zr,
+    ys,
+    yr,
+    ls,
+    lr,
+    hs,
+    hr,
 ):
     nz, ny, nx = geo
     no = 2 * nx
@@ -188,6 +200,7 @@
     own = xi * 2 + core
     tp_other = tp + 1 - 2 * core
     tp_half = tp + 2 - 4 * zh
+    tp_odd = tp + 1 - core
 
     def o_tp(d):
         o = (own + d) % no
@@ -200,6 +213,7 @@
         return zi * ny + (yi + e) % ny
 
     partners = [(z_rep(d), tp) for d in range(1, nz)]
+    partners += [(z_rep(d), tp_other) for d in range(1, nz)]
     partners += [(y_rep(e), tp) for e in range(1, ny)]
     partners += [(y_rep(e), tp_other) for e in range(1, ny)]
     partners += [(rep, o_tp(d)) for d in range(1, no)]
@@ -260,6 +274,80 @@
         used.append(copy)
         return copy
 
+    def link(src, dst, send_sem, recv_sem, device):
+        return pltpu.make_async_remote_copy(
+            src_ref=src,
+            dst_ref=dst,
+            send_sem=send_sem,
+            recv_sem=recv_sem,
+            device_id=device,
+            device_id_type=pl.DeviceIdType.MESH,
+        )
+
+    even, odd_core = pl.when(core == 0), pl.when(core == 1)
+
+    def z_copy(k, item, gather, c, d):
+        return link(item, gather.at[c, d], zs.at[k, d], zr.at[k, c, d], (z_rep(d), tp_odd))
+
+    def y_copy(k, stage, land, c, e):
+        return link(
+            stage.at[c, e], land.at[e], ys.at[k, c, e], yr.at[k, e], (y_rep(e), tp_odd - 1 + c)
+        )
+
+    def late_copy(c, d):
+        device = (rep, ((xi + d) % nx) * 4 + zh * 2 + 1)
+        return link(late_send, late_land.at[c, d], ls.at[d], lr.at[c, d], device)
+
+    def set_out(k, item, gather):
+        for d in range(1, nz):
+            z_copy(k, item, gather, core, d).start()
+
+        @even
+        def _():
+            z_copy(k, item, gather, 0, 0).start()
+
+        @odd_core
+        def _():
+            gather[1, 0] = item[...]
+
+    def turn(k, item, gather, stage, land, chooser):
+        @odd_core
+        def _():
+            for c in range(2):
+                for d in range(nz):
+                    if (c, d) != (1, 0):
+                        z_copy(k, item, gather, c, d).wait_recv()
+                chosen = nn(chooser, gather[c].reshape(nz * 16, 256)).astype(BF16)
+                for e in range(ny):
+                    stage[c, e] = chosen[e * 16 : (e + 1) * 16]
+                    if (c, e) != (1, 0):
+                        y_copy(k, stage, land, c, e).start()
+                    else:
+                        land[0] = chosen[0:16]
+
+    def arrive(k, stage, land):
+        for e in range(1, ny):
+            y_copy(k, stage, land, 0, e).wait_recv()
+
+        @even
+        def _():
+            y_copy(k, stage, land, 0, 0).wait_recv()
+
+    def drain(k, item, gather, stage, land):
+        for d in range(1, nz):
+            z_copy(k, item, gather, core, d).wait_send()
+
+        @even
+        def _():
+            z_copy(k, item, gather, 0, 0).wait_send()
+
+        @odd_core
+        def _():
+            for c in range(2):
+                for e in range(ny):
+                    if (c, e) != (1, 0):
+                        y_copy(k, stage, land, c, e).wait_send()
+
     need("src_ref")
     src = src_ref[...]
     lane_n = iota((1, n), 1)
@@ -293,13 +381,13 @@
             )
             blocks.append(jnp.concatenate([x_s[:, b * 256 : (b + 1) * 256], side], axis=1))
     item = nn(pack, jnp.concatenate(blocks, axis=0)).astype(BF16)
-    gather_x[0] = item[:, 0:256]
+    item_x[...] = item[:, 0:256]
     gather_q[0] = item[:, 256:512]
 
     pl.semaphore_wait(barrier, len(partners))
     pl.semaphore_signal(ready, inc=1, device_id=mirror, device_id_type=pl.DeviceIdType.MESH)
 
-    z_x = [push(gather_x.at[0], gather_x.at[d], (z_rep(d), tp)) for d in range(1, nz)]
+    set_out(0, item_x, gather_x)
     z_q = [push(gather_q.at[0], gather_q.at[d], (z_rep(d), tp)) for d in range(1, nz)]
     q_swap = push(q_ref, q_other, (rep, tp_other))
     nk_swap = push(nk_ref, nk_other, (rep, tp_other))
@@ -357,7 +445,7 @@
         landing[0] = chosen[0:16]
         return [push(staged.at[e], landing.at[e], (y_rep(e), tp)) for e in range(1, ny)]
 
-    y_x = select(z_x, select_in, gather_x, stage_x, land_x)
+    turn(0, item_x, gather_x, stage_x, land_x, select_in)
 
     for copy in part_out:
         copy.wait_recv()
@@ -406,8 +494,7 @@
     mask_ref[...] = allowed.astype(BF16)
     bias_ref[...] = jnp.where(allowed > 0.5, 0.0, MASKED)
 
-    for copy in y_x:
-        copy.wait_recv()
+    arrive(0, stage_x, land_x)
     er = iota((128, ny * 16), 0)
     ec = iota((128, ny * 16), 1)
     wanted_step = jnp.where(er < 64, er & 1, 0)
@@ -435,7 +522,13 @@
         [by_quarter([main[:, b * 128 : (b + 1) * 128] for b in range(4)]), tail], axis=1
     )
     late_send[...] = late_own.astype(BF16)
-    late_out = [push(late_send, late_land.at[d], (rep, o_tp(d))) for d in range(1, no)]
+    for d in range(1, nx):
+        late_copy(core, d).start()
+
+    @even
+    def _():
+        late_copy(0, 0).start()
+
 
     need("pool")
     q_swap.wait_recv()
@@ -483,13 +576,20 @@
 
     take(own, packed)
 
-    for copy in late_out:
-        copy.wait_recv()
-    late_sum = late_own
-    for d in range(1, no):
-        late_sum = late_sum + late_land[d].astype(F32)
-    late_half[...] = late_sum.astype(BF16)
-    late_swap = push(late_half, late_half_land, (rep, tp_half))
+    late_swap = link(late_half, late_half_land, hs.at[0], hr.at[0], (rep, tp_half))
+    late_over = link(late_total, late_total, hs.at[1], hr.at[1], (rep, tp_odd - 1))
+
+    @odd_core
+    def _():
+        late_sum = late_own
+        for c in range(2):
+            for d in range(nx):
+                if (c, d) != (1, 0):
+                    late_copy(c, d).wait_recv()
+                    late_sum = late_sum + late_land[c, d].astype(F32)
+        late_acc[...] = late_sum
+        late_half[...] = late_sum.astype(BF16)
+        late_swap.start()
 
     for copy in y_q:
         copy.wait_recv()
@@ -579,8 +679,17 @@
     gather_a[0] = heads.astype(BF16)
     z_a = [push(gather_a.at[0], gather_a.at[d], (z_rep(d), tp)) for d in range(1, nz)]
 
-    late_swap.wait_recv()
-    late_sum = late_sum + late_half_land[...].astype(F32)
+    @odd_core
+    def _():
+        late_swap.wait_recv()
+        late_total[...] = late_acc[...] + late_half_land[...].astype(F32)
+        late_over.start()
+
+    @even
+    def _():
+        late_over.wait_recv()
+
+    late_sum = late_total[...]
     main = late_sum[:, 0:128]
     square = jnp.broadcast_to(jnp.sum(main * main, axis=1, keepdims=True), (16, 128))
     square = square + pltpu.roll(square, 8, 0)
@@ -616,10 +725,10 @@
                 state, late_dt[m : m + 1], late_act[m : m + 1], late_tail[m : m + 1]
             )
             late_mixed = jnp.where(rows == m, out, late_mixed)
-    gather_m[0] = by_quarter(
+    item_m[...] = by_quarter(
         [late_mixed[:, b * 256 : (b + 1) * 256] for b in range(4)]
     ).astype(BF16)
-    z_m = [push(gather_m.at[0], gather_m.at[d], (z_rep(d), tp)) for d in range(1, nz)]
+    set_out(1, item_m, gather_m)
 
     scan(2, mid, False)
     need("z_ref")
@@ -643,9 +752,10 @@
         & ((fr >> 6) == (fc & 1))
         & (nt(slot_pick, hot(home == own_code)) > 0.5)
     )
-    y_m = select(z_m, select_out, gather_m, stage_m, land_m)
-    for copy in y_a + y_m:
+    turn(1, item_m, gather_m, stage_m, land_m, select_out)
+    for copy in y_a:
         copy.wait_recv()
+    arrive(1, stage_m, land_m)
     returned = nn(put, land_m[...].reshape(ny * 16, 256))
     attended = nn(put, land_a[...].reshape(ny * 16, 128))
     for s in (2, 3):
@@ -658,6 +768,19 @@
 
     for copy in used:
         copy.wait_send()
+    drain(0, item_x, gather_x, stage_x, land_x)
+    drain(1, item_m, gather_m, stage_m, land_m)
+    for d in range(1, nx):
+        late_copy(core, d).wait_send()
+
+    @even
+    def _():
+        late_copy(0, 0).wait_send()
+
+    @odd_core
+    def _():
+        late_swap.wait_send()
+        late_over.wait_send()
 
 
 def shards(
@@ -686,7 +809,7 @@
     nz, ny, nx = geo
     no = 2 * nx
     rpo = 64 // no
-    copies = 4 * (nz - 1) + 4 * (ny - 1) + ny + 3 * (no - 1) + 6
+    copies = 2 * (nz - 1) + 2 * (ny - 1) + ny + 2 * (no - 1) + 5
     operands = (
         slot_source.reshape(1, -1),
         queries,
@@ -721,8 +844,9 @@
         pltpu.VMEM((4, 16, 1024), F32),
         pltpu.VMEM((64, 512), F32),
         pltpu.VMEM((64, 128), F32),
-        pltpu.VMEM((nz, 16, 256), BF16),
-        pltpu.VMEM((ny, 16, 256), BF16),
+        pltpu.VMEM((16, 256), BF16),
+        pltpu.VMEM((2, nz, 16, 256), BF16),
+        pltpu.VMEM((2, ny, 16, 256), BF16),
         pltpu.VMEM((ny, 16, 256), BF16),
         pltpu.VMEM((nz, 16, 256), BF16),
         pltpu.VMEM((ny, 16, 256), BF16),
@@ -740,13 +864,16 @@
         pltpu.VMEM((256, 256), F32),
         pltpu.VMEM((256, 256), F32),
         pltpu.VMEM((16, 256), BF16),
-        pltpu.VMEM((no, 16, 256), BF16),
+        pltpu.VMEM((2, nx, 16, 256), BF16),
         pltpu.VMEM((16, 256), BF16),
         pltpu.VMEM((16, 256), BF16),
+        pltpu.VMEM((16, 256), F32),
+        pltpu.VMEM((16, 256), F32),
         pltpu.VMEM((32, 256), F32),
         pltpu.VMEM((32, 256), F32),
-        pltpu.VMEM((nz, 16, 256), BF16),
-        pltpu.VMEM((ny, 16, 256), BF16),
+        pltpu.VMEM((16, 256), BF16),
+        pltpu.VMEM((2, nz, 16, 256), BF16),
+        pltpu.VMEM((2, ny, 16, 256), BF16),
         pltpu.VMEM((ny, 16, 256), BF16),
         pltpu.VMEM((nz, 16, 128), BF16),
         pltpu.VMEM((ny, 16, 128), BF16),
@@ -757,6 +884,14 @@
         pltpu.SemaphoreType.DMA((copies,)),
         pltpu.SemaphoreType.DMA((len(operands),)),
         pltpu.SemaphoreType.REGULAR,
+        pltpu.SemaphoreType.DMA((2, nz)),
+        pltpu.SemaphoreType.DMA((2, 2, nz)),
+        pltpu.SemaphoreType.DMA((2, 2, ny)),
+        pltpu.SemaphoreType.DMA((2, ny)),
+        pltpu.SemaphoreType.DMA((nx,)),
+        pltpu.SemaphoreType.DMA((2, nx)),
+        pltpu.SemaphoreType.DMA((2,)),
+        pltpu.SemaphoreType.DMA((2,)),
     ]
     return pl.pallas_call(
         functools.partial(kernel, geo),

time: 51.2 us -> 51.5 us (level); the launches traced: 50.5 us -> 51.4 us
  Pallas kernels: 48.6 us -> 49.5 us
    pallas_call x1, Pallas kernels: 48.6 us -> 49.5 us  [shards(): pl.pallas_call(functools.partial(kernel, geo), out_shape=(pltpu.VMEM(quer...]
where the time goes in v4:
time: 51.5 us; the launch traced here: 51.4 us
  Pallas kernels  49.5 us (96%)
  local copies, waits for them, and re-layouts  1.29 us (3%)
  between operations  0.65 us (1%)
    pallas_call x1, Pallas kernels, shards(): pl.pallas_call(functools.partial(kernel, geo), out_shape=(pltpu.VMEM(quer...  49.5 us
    unnamed x2, local copies, waits for them, and re-layouts  1.29 us

profile of v4, /device:TPU:1, one launch (start us, length us, event | category | flops | bytes accessed | tf_op | source)
XLA Modules:
  0.0 51.4 jit_solution(5026527935007347021)
XLA Ops:
  0.6 49.5 %shard_map.203 = (bf16[4,16,512]{2,1,0:T(8,128)(2,1)S(1)}, bf16[4,16,1024]{2,1,0:T(8,128)(2,1)S(1)}) custom-call(s32[1,512]{1,0:T(1,128)} %bitcast.11, bf16[4,16,512]{2,1,0:T(8,128)(2,1)} %q_ref_h.1, bf16[4,16,128]{2,1,0:T(8,128)(2,1)} %nk_ref_h.1, bf16[4,16,1024]{2,1,0:T(8,128)(2,1)} %x_ref_h.1, s32[512]{0:T(512)} %src_s_h.1, ...), custom_call_target="tpu_custom_call" | custom-call | tf_op jit(solution)/shard_map/pallas_call | solution.py:896
  50.1 0.6 %copy.24 = bf16[4,16,512]{2,1,0:T(8,128)(2,1)} copy(bf16[4,16,512]{2,1,0:T(8,128)(2,1)S(1)} %get-tuple-element.2) | data formatting | bytes 131072
  50.7 0.7 %copy.25 = bf16[4,16,1024]{2,1,0:T(8,128)(2,1)} copy(bf16[4,16,1024]{2,1,0:T(8,128)(2,1)S(1)} %get-tuple-element.3) | data formatting | bytes 262144

commit v5 on v4

--- a/solution.py
+++ b/solution.py
@@ -313,7 +313,7 @@
     def turn(k, item, gather, stage, land, chooser):
         @odd_core
         def _():
-            for c in range(2):
+            for c in (1, 0):
                 for d in range(nz):
                     if (c, d) != (1, 0):
                         z_copy(k, item, gather, c, d).wait_recv()
@@ -384,14 +384,6 @@
     item_x[...] = item[:, 0:256]
     gather_q[0] = item[:, 256:512]
 
-    pl.semaphore_wait(barrier, len(partners))
-    pl.semaphore_signal(ready, inc=1, device_id=mirror, device_id_type=pl.DeviceIdType.MESH)
-
-    set_out(0, item_x, gather_x)
-    z_q = [push(gather_q.at[0], gather_q.at[d], (z_rep(d), tp)) for d in range(1, nz)]
-    q_swap = push(q_ref, q_other, (rep, tp_other))
-    nk_swap = push(nk_ref, nk_other, (rep, tp_other))
-
     need("conv_ref", "cw_ref", "cb_ref")
     window = [conv_ref[w].astype(F32) for w in range(3)] + [x_ref[s].astype(F32) for s in range(4)]
     conv_last = window[2].astype(BF16)
@@ -415,9 +407,16 @@
     for o in range(no):
         part[o, :, 0:512] = main[o * rpo : (o + 1) * rpo]
         part[o, :, 512:640] = tail[o * rpo : (o + 1) * rpo]
+    pl.semaphore_wait(barrier, len(partners))
+    pl.semaphore_signal(ready, inc=1, device_id=mirror, device_id_type=pl.DeviceIdType.MESH)
+
+    set_out(0, item_x, gather_x)
     part_out = [
         push(part.at[(own + d) % no], part_land.at[d], (rep, o_tp(d))) for d in range(1, no)
     ]
+    z_q = [push(gather_q.at[0], gather_q.at[d], (z_rep(d), tp)) for d in range(1, nz)]
+    q_swap = push(q_ref, q_other, (rep, tp_other))
+    nk_swap = push(nk_ref, nk_other, (rep, tp_other))
 
     same = iota((n, n), 0)
     lane_nn = iota((n, n), 1)
@@ -445,8 +444,6 @@
         landing[0] = chosen[0:16]
         return [push(staged.at[e], landing.at[e], (y_rep(e), tp)) for e in range(1, ny)]
 
-    turn(0, item_x, gather_x, stage_x, land_x, select_in)
-
     for copy in part_out:
         copy.wait_recv()
     summed = part[own]
@@ -468,6 +465,8 @@
         return jnp.concatenate([v[:rpo, 0:256], v[rpo:, 0:256], v[:rpo, 256:384]], axis=1)
 
     half_send[...] = pack_half(summed)
+
+    turn(0, item_x, gather_x, stage_x, land_x, select_in)
     pl.semaphore_wait(ready, 1)
     half = push(half_send, half_land, (rep, tp_half))
 
@@ -493,42 +492,6 @@
         )
     mask_ref[...] = allowed.astype(BF16)
     bias_ref[...] = jnp.where(allowed > 0.5, 0.0, MASKED)
-
-    arrive(0, stage_x, land_x)
-    er = iota((128, ny * 16), 0)
-    ec = iota((128, ny * 16), 1)
-    wanted_step = jnp.where(er < 64, er & 1, 0)
-    expand = hot(
-        (((er >> 4) & 3) == ((ec >> 2) & 3))
-        & (((er >> 1) & 1) == ((ec >> 1) & 1))
-        & (wanted_step == (ec & 1))
-    )
-    arrived = nn(expand, land_x[...].reshape(ny * 16, 256))
-    x_now = jnp.concatenate([arrived[b * 16 : (b + 1) * 16] for b in range(4)], axis=1)
-    x_prev = jnp.concatenate(
-        [arrived[64 + b * 16 : 64 + (b + 1) * 16] for b in range(4)], axis=1
-    )
-    last_row = nn(pick16, conv_last)
-    x_zero = nn(pick16, x_ref[0])
-    x_one = nn(pick16, x_ref[1])
-    odd = (iota((16, 1024), 0) & 1) == 1
-    total = jnp.where(odd, x_zero, last_row) * cw[0:1]
-    total = total + jnp.where(odd, x_one, x_zero) * cw[1:2]
-    total = total + jnp.where(odd, x_prev, x_one) * cw[2:3]
-    total = total + x_now * cw[3:4]
-    late_act = silu(total + cb)
-    main, tail = project(late_act.astype(BF16))
-    late_own = jnp.concatenate(
-        [by_quarter([main[:, b * 128 : (b + 1) * 128] for b in range(4)]), tail], axis=1
-    )
-    late_send[...] = late_own.astype(BF16)
-    for d in range(1, nx):
-        late_copy(core, d).start()
-
-    @even
-    def _():
-        late_copy(0, 0).start()
-
 
     need("pool")
     q_swap.wait_recv()
@@ -547,34 +510,54 @@
     )
     bias16 = bias_ref[...]
     bias = jnp.concatenate([bias16] * 16, axis=0)
-    for source, target in ((q_other, away), (q_ref, near)):
+    def attend_all(source, target):
         rows = jnp.concatenate(
             [source[s][:, h * 128 : (h + 1) * 128] for s in range(4) for h in range(4)], axis=0
         )
         out, stats = attend(rows, keys, values, extra_keys, extra_values, bias, extra_bias)
         target[:, 0:128] = out
         target[:, 128:256] = stats
-        if target is away:
-            partial = push(away, far, (rep, tp_other))
-
-    need("dtg_ref")
-    half.wait_recv()
-    summed = summed + unpack_half(half_land[...])
-    main = summed[:, 0:512]
-    mean = jnp.sum(main * main, axis=1, keepdims=True) / 512.0
-    low = main * lax.rsqrt(mean + EPS) * dtg_ref[...]
-    normed = jnp.concatenate([low, tail_norm(summed[:, 512:640])], axis=1)
-    packed = pack_half(normed)
-    norm_send[...] = packed
-    norm_out = [push(norm_send, norm_land.at[d], (rep, o_tp(d))) for d in range(1, no)]
-
-    def take(o, v):
-        v = unpack_half(v)
-        start = pl.multiple_of(o * rpo, rpo)
-        dtl[pl.ds(start, rpo), :] = v[:, 0:512]
-        tails[pl.ds(start, rpo), :] = v[:, 512:640]
-
-    take(own, packed)
+
+    attend_all(q_other, away)
+    partial = push(away, far, (rep, tp_other))
+
+    arrive(0, stage_x, land_x)
+    er = iota((128, ny * 16), 0)
+    ec = iota((128, ny * 16), 1)
+    wanted_step = jnp.where(er < 64, er & 1, 0)
+    expand = hot(
+        (((er >> 4) & 3) == ((ec >> 2) & 3))
+        & (((er >> 1) & 1) == ((ec >> 1) & 1))
+        & (wanted_step == (ec & 1))
+    )
+    arrived = nn(expand, land_x[...].reshape(ny * 16, 256))
+    x_now = jnp.concatenate([arrived[b * 16 : (b + 1) * 16] for b in range(4)], axis=1)
+    x_prev = jnp.concatenate(
+        [arrived[64 + b * 16 : 64 + (b + 1) * 16] for b in range(4)], axis=1
+    )
+    last_row = nn(pick16, conv_last)
+    x_zero = nn(pick16, x_ref[0])
+    x_one = nn(pick16, x_ref[1])
+    odd = (iota((16, 1024), 0) & 1) == 1
+    total = jnp.where(odd, x_zero, last_row) * cw[0:1]
+    total = total + jnp.where(odd, x_one, x_zero) * cw[1:2]
+    total = total + jnp.where(odd, x_prev, x_one) * cw[2:3]
+    total = total + x_now * cw[3:4]
+    late_act = silu(total + cb)
+    main, tail = project(late_act.astype(BF16))
+    late_own = jnp.concatenate(
+        [by_quarter([main[:, b * 128 : (b + 1) * 128] for b in range(4)]), tail], axis=1
+    )
+    late_send[...] = late_own.astype(BF16)
+    for d in range(1, nx):
+        late_copy(core, d).start()
+
+    @even
+    def _():
+        late_copy(0, 0).start()
+
+
+    attend_all(q_ref, near)
 
     late_swap = link(late_half, late_half_land, hs.at[0], hr.at[0], (rep, tp_half))
     late_over = link(late_total, late_total, hs.at[1], hr.at[1], (rep, tp_odd - 1))
@@ -590,6 +573,25 @@
         late_acc[...] = late_sum
         late_half[...] = late_sum.astype(BF16)
         late_swap.start()
+
+    need("dtg_ref")
+    half.wait_recv()
+    summed = summed + unpack_half(half_land[...])
+    main = summed[:, 0:512]
+    mean = jnp.sum(main * main, axis=1, keepdims=True) / 512.0
+    low = main * lax.rsqrt(mean + EPS) * dtg_ref[...]
+    normed = jnp.concatenate([low, tail_norm(summed[:, 512:640])], axis=1)
+    packed = pack_half(normed)
+    norm_send[...] = packed
+    norm_out = [push(norm_send, norm_land.at[d], (rep, o_tp(d))) for d in range(1, no)]
+
+    def take(o, v):
+        v = unpack_half(v)
+        start = pl.multiple_of(o * rpo, rpo)
+        dtl[pl.ds(start, rpo), :] = v[:, 0:512]
+        tails[pl.ds(start, rpo), :] = v[:, 512:640]
+
+    take(own, packed)
 
     for copy in y_q:
         copy.wait_recv()
@@ -734,16 +736,18 @@
     need("z_ref")
     partial.wait_recv()
     kept = []
+    gates = []
     for s in range(4):
+        gate = silu(z_ref[s].astype(F32))
         block = combine(near[s * 64 : (s + 1) * 64, :], far[s * 64 : (s + 1) * 64, :])
         block = jnp.concatenate([block[h * 16 : (h + 1) * 16] for h in range(4)], axis=1)
         if s < 2:
             attn_ref[s] = block.astype(BF16)
-            mix_ref[s] = (mixed[s] * silu(z_ref[s].astype(F32))).astype(BF16)
+            mix_ref[s] = (mixed[s] * gate).astype(BF16)
         else:
             kept.append(block)
-
-    y_a = select(z_a, select_out, gather_a, stage_a, land_a)
+            gates.append((gate, mixed[s] * gate))
+
     own_code = rep * 2 + ((iota((ny * 16, n), 0) >> 1) & 1)
     fr = iota((128, ny * 16), 0)
     fc = iota((128, ny * 16), 1)
@@ -753,18 +757,20 @@
         & (nt(slot_pick, hot(home == own_code)) > 0.5)
     )
     turn(1, item_m, gather_m, stage_m, land_m, select_out)
+    y_a = select(z_a, select_out, gather_a, stage_a, land_a)
+    spots = [[s * 64 + b * 16 for b in range(4)] for s in range(2)]
     for copy in y_a:
         copy.wait_recv()
+    attended = nn(put, land_a[...].reshape(ny * 16, 128))
+    for s in range(2):
+        back = jnp.concatenate([attended[p : p + 16] for p in spots[s]], axis=1)
+        attn_ref[s + 2] = jnp.where(foreign_col, back, kept[s]).astype(BF16)
     arrive(1, stage_m, land_m)
     returned = nn(put, land_m[...].reshape(ny * 16, 256))
-    attended = nn(put, land_a[...].reshape(ny * 16, 128))
-    for s in (2, 3):
-        spots = [(s - 2) * 64 + b * 16 for b in range(4)]
-        back = jnp.concatenate([returned[p : p + 16] for p in spots], axis=1)
-        whole = jnp.where(foreign_col, back, mixed[s])
-        mix_ref[s] = (whole * silu(z_ref[s].astype(F32))).astype(BF16)
-        back = jnp.concatenate([attended[p : p + 16] for p in spots], axis=1)
-        attn_ref[s] = jnp.where(foreign_col, back, kept[s - 2]).astype(BF16)
+    for s in range(2):
+        back = jnp.concatenate([returned[p : p + 16] for p in spots[s]], axis=1)
+        gate, own_mix = gates[s]
+        mix_ref[s + 2] = jnp.where(foreign_col, back * gate, own_mix).astype(BF16)
 
     for copy in used:
         copy.wait_send()

time: 51.5 us -> 51.6 us (level)
  no operation moved by 1% of the time
where the time goes in v5:
time: 51.6 us; the launch traced here: 51.5 us
  Pallas kernels  49.6 us (96%)
  local copies, waits for them, and re-layouts  1.29 us (2%)
  between operations  0.65 us (1%)
    pallas_call x1, Pallas kernels, shards(): pl.pallas_call(functools.partial(kernel, geo), out_shape=(pltpu.VMEM(quer...  49.6 us
    unnamed x2, local copies, waits for them, and re-layouts  1.29 us

profile of v5, /device:TPU:1, one launch (start us, length us, event | category | flops | bytes accessed | tf_op | source)
XLA Modules:
  0.0 51.5 jit_solution(6834599266099983774)
XLA Ops:
  0.6 49.6 %shard_map.203 = (bf16[4,16,512]{2,1,0:T(8,128)(2,1)S(1)}, bf16[4,16,1024]{2,1,0:T(8,128)(2,1)S(1)}) custom-call(s32[1,512]{1,0:T(1,128)} %bitcast.11, bf16[4,16,512]{2,1,0:T(8,128)(2,1)} %q_ref_h.1, bf16[4,16,128]{2,1,0:T(8,128)(2,1)} %nk_ref_h.1, bf16[4,16,1024]{2,1,0:T(8,128)(2,1)} %x_ref_h.1, s32[512]{0:T(512)} %src_s_h.1, ...), custom_call_target="tpu_custom_call" | custom-call | tf_op jit(solution)/shard_map/pallas_call | solution.py:902
  50.2 0.6 %copy.24 = bf16[4,16,512]{2,1,0:T(8,128)(2,1)} copy(bf16[4,16,512]{2,1,0:T(8,128)(2,1)S(1)} %get-tuple-element.2) | data formatting | bytes 131072
  50.9 0.7 %copy.25 = bf16[4,16,1024]{2,1,0:T(8,128)(2,1)} copy(bf16[4,16,1024]{2,1,0:T(8,128)(2,1)S(1)} %get-tuple-element.3) | data formatting | bytes 262144

commit v6 on v3

--- a/solution.py
+++ b/solution.py
@@ -260,6 +260,15 @@
         used.append(copy)
         return copy
 
+    def send_all(src, land, devices):
+        return [push(src, land.at[d], device) for d, device in devices]
+
+    far_z = sorted(range(1, nz), key=lambda d: min(d, nz - d))
+    far_y = sorted(range(1, ny), key=lambda e: -min(e, ny - e))
+    far_o = sorted(range(1, no), key=lambda d: -min(d, no - d))
+    columns_z = [(d, (z_rep(d), tp)) for d in far_z]
+    peers = [(d, (rep, o_tp(d))) for d in far_o]
+
     need("src_ref")
     src = src_ref[...]
     lane_n = iota((1, n), 1)
@@ -296,14 +305,6 @@
     gather_x[0] = item[:, 0:256]
     gather_q[0] = item[:, 256:512]
 
-    pl.semaphore_wait(barrier, len(partners))
-    pl.semaphore_signal(ready, inc=1, device_id=mirror, device_id_type=pl.DeviceIdType.MESH)
-
-    z_x = [push(gather_x.at[0], gather_x.at[d], (z_rep(d), tp)) for d in range(1, nz)]
-    z_q = [push(gather_q.at[0], gather_q.at[d], (z_rep(d), tp)) for d in range(1, nz)]
-    q_swap = push(q_ref, q_other, (rep, tp_other))
-    nk_swap = push(nk_ref, nk_other, (rep, tp_other))
-
     need("conv_ref", "cw_ref", "cb_ref")
     window = [conv_ref[w].astype(F32) for w in range(3)] + [x_ref[s].astype(F32) for s in range(4)]
     conv_last = window[2].astype(BF16)
@@ -327,9 +328,16 @@
     for o in range(no):
         part[o, :, 0:512] = main[o * rpo : (o + 1) * rpo]
         part[o, :, 512:640] = tail[o * rpo : (o + 1) * rpo]
+    pl.semaphore_wait(barrier, len(partners))
+    pl.semaphore_signal(ready, inc=1, device_id=mirror, device_id_type=pl.DeviceIdType.MESH)
+
+    z_x = send_all(gather_x.at[0], gather_x, columns_z)
     part_out = [
         push(part.at[(own + d) % no], part_land.at[d], (rep, o_tp(d))) for d in range(1, no)
     ]
+    z_q = send_all(gather_q.at[0], gather_q, columns_z)
+    q_swap = push(q_ref, q_other, (rep, tp_other))
+    nk_swap = push(nk_ref, nk_other, (rep, tp_other))
 
     same = iota((n, n), 0)
     lane_nn = iota((n, n), 1)
@@ -355,9 +363,7 @@
         for e in range(ny):
             staged[e] = chosen[e * 16 : (e + 1) * 16]
         landing[0] = chosen[0:16]
-        return [push(staged.at[e], landing.at[e], (y_rep(e), tp)) for e in range(1, ny)]
-
-    y_x = select(z_x, select_in, gather_x, stage_x, land_x)
+        return [push(staged.at[e], landing.at[e], (y_rep(e), tp)) for e in far_y]
 
     for copy in part_out:
         copy.wait_recv()
@@ -380,6 +386,8 @@
         return jnp.concatenate([v[:rpo, 0:256], v[rpo:, 0:256], v[:rpo, 256:384]], axis=1)
 
     half_send[...] = pack_half(summed)
+
+    y_x = select(z_x, select_in, gather_x, stage_x, land_x)
     pl.semaphore_wait(ready, 1)
     half = push(half_send, half_land, (rep, tp_half))
 
@@ -405,37 +413,6 @@
         )
     mask_ref[...] = allowed.astype(BF16)
     bias_ref[...] = jnp.where(allowed > 0.5, 0.0, MASKED)
-
-    for copy in y_x:
-        copy.wait_recv()
-    er = iota((128, ny * 16), 0)
-    ec = iota((128, ny * 16), 1)
-    wanted_step = jnp.where(er < 64, er & 1, 0)
-    expand = hot(
-        (((er >> 4) & 3) == ((ec >> 2) & 3))
-        & (((er >> 1) & 1) == ((ec >> 1) & 1))
-        & (wanted_step == (ec & 1))
-    )
-    arrived = nn(expand, land_x[...].reshape(ny * 16, 256))
-    x_now = jnp.concatenate([arrived[b * 16 : (b + 1) * 16] for b in range(4)], axis=1)
-    x_prev = jnp.concatenate(
-        [arrived[64 + b * 16 : 64 + (b + 1) * 16] for b in range(4)], axis=1
-    )
-    last_row = nn(pick16, conv_last)
-    x_zero = nn(pick16, x_ref[0])
-    x_one = nn(pick16, x_ref[1])
-    odd = (iota((16, 1024), 0) & 1) == 1
-    total = jnp.where(odd, x_zero, last_row) * cw[0:1]
-    total = total + jnp.where(odd, x_one, x_zero) * cw[1:2]
-    total = total + jnp.where(odd, x_prev, x_one) * cw[2:3]
-    total = total + x_now * cw[3:4]
-    late_act = silu(total + cb)
-    main, tail = project(late_act.astype(BF16))
-    late_own = jnp.concatenate(
-        [by_quarter([main[:, b * 128 : (b + 1) * 128] for b in range(4)]), tail], axis=1
-    )
-    late_send[...] = late_own.astype(BF16)
-    late_out = [push(late_send, late_land.at[d], (rep, o_tp(d))) for d in range(1, no)]
 
     need("pool")
     q_swap.wait_recv()
@@ -454,15 +431,57 @@
     )
     bias16 = bias_ref[...]
     bias = jnp.concatenate([bias16] * 16, axis=0)
-    for source, target in ((q_other, away), (q_ref, near)):
+    def attend_all(source, target):
         rows = jnp.concatenate(
             [source[s][:, h * 128 : (h + 1) * 128] for s in range(4) for h in range(4)], axis=0
         )
         out, stats = attend(rows, keys, values, extra_keys, extra_values, bias, extra_bias)
         target[:, 0:128] = out
         target[:, 128:256] = stats
-        if target is away:
-            partial = push(away, far, (rep, tp_other))
+
+    attend_all(q_other, away)
+    partial = push(away, far, (rep, tp_other))
+
+    er = iota((128, ny * 16), 0)
+    ec = iota((128, ny * 16), 1)
+    wanted_step = jnp.where(er < 64, er & 1, 0)
+    expand = hot(
+        (((er >> 4) & 3) == ((ec >> 2) & 3))
+        & (((er >> 1) & 1) == ((ec >> 1) & 1))
+        & (wanted_step == (ec & 1))
+    )
+    last_row = nn(pick16, conv_last)
+    x_zero = nn(pick16, x_ref[0])
+    x_one = nn(pick16, x_ref[1])
+    odd = (iota((16, 1024), 0) & 1) == 1
+    known = jnp.where(odd, x_zero, last_row) * cw[0:1]
+    known = known + jnp.where(odd, x_one, x_zero) * cw[1:2]
+    known = known + jnp.where(odd, 0.0, x_one) * cw[2:3]
+    for copy in y_x:
+        copy.wait_recv()
+    arrived = nn(expand, land_x[...].reshape(ny * 16, 256))
+    x_now = jnp.concatenate([arrived[b * 16 : (b + 1) * 16] for b in range(4)], axis=1)
+    x_prev = jnp.concatenate(
+        [arrived[64 + b * 16 : 64 + (b + 1) * 16] for b in range(4)], axis=1
+    )
+    total = known + jnp.where(odd, x_prev, 0.0) * cw[2:3] + x_now * cw[3:4]
+    late_act = silu(total + cb)
+    main, tail = project(late_act.astype(BF16))
+    late_own = jnp.concatenate(
+        [by_quarter([main[:, b * 128 : (b + 1) * 128] for b in range(4)]), tail], axis=1
+    )
+    late_send[...] = late_own.astype(BF16)
+    late_out = send_all(late_send, late_land, peers)
+
+    attend_all(q_ref, near)
+
+    for copy in late_out:
+        copy.wait_recv()
+    late_sum = late_own
+    for d in range(1, no):
+        late_sum = late_sum + late_land[d].astype(F32)
+    late_half[...] = late_sum.astype(BF16)
+    late_swap = push(late_half, late_half_land, (rep, tp_half))
 
     need("dtg_ref")
     half.wait_recv()
@@ -482,14 +501,6 @@
         tails[pl.ds(start, rpo), :] = v[:, 512:640]
 
     take(own, packed)
-
-    for copy in late_out:
-        copy.wait_recv()
-    late_sum = late_own
-    for d in range(1, no):
-        late_sum = late_sum + late_land[d].astype(F32)
-    late_half[...] = late_sum.astype(BF16)
-    late_swap = push(late_half, late_half_land, (rep, tp_half))
 
     for copy in y_q:
         copy.wait_recv()
@@ -531,7 +542,7 @@
     late_away[...] = jnp.concatenate([out[32:64], stats[32:64]], axis=1)
     late_partial = push(late_away, late_far, (rep, tp_other))
 
-    for d, copy in enumerate(norm_out, 1):
+    for d, copy in zip(range(1, no), norm_out):
         copy.wait_recv()
         take((own - d + no) % no, norm_land[d])
     need("dw", "dtb_ref", "bg_ref", "cg_ref", "skip_ref", "a_ref", "ssm")
@@ -579,25 +590,14 @@
     gather_a[0] = heads.astype(BF16)
     z_a = [push(gather_a.at[0], gather_a.at[d], (z_rep(d), tp)) for d in range(1, nz)]
 
-    late_swap.wait_recv()
-    late_sum = late_sum + late_half_land[...].astype(F32)
-    main = late_sum[:, 0:128]
-    square = jnp.broadcast_to(jnp.sum(main * main, axis=1, keepdims=True), (16, 128))
-    square = square + pltpu.roll(square, 8, 0)
-    square = square + pltpu.roll(square, 4, 0)
+    need("src_s")
     gain = dtg_ref[...]
     gains = by_quarter(
         [jnp.broadcast_to(gain[:, b * 128 : (b + 1) * 128], (16, 128)) for b in range(4)]
     )
-    low = (main * lax.rsqrt(square / 512.0 + EPS) * gains).astype(BF16)
     wr = iota((64, 16), 0)
     wc = iota((64, 16), 1)
-    spread = nn(hot(((wr >> 4) == (wc >> 2)) & ((wr & 3) == (wc & 3))), low)
-    low = jnp.concatenate([spread[b * 16 : (b + 1) * 16] for b in range(4)], axis=1)
-    late_dt = softplus(nn(low.astype(BF16), dw[...]) + dtb_ref[...])
-    late_tail = tail_norm(late_sum[:, 128:256])
-
-    need("src_s")
+    widen = hot(((wr >> 4) == (wc >> 2)) & ((wr & 3) == (wc & 3)))
     base = rep * 16
     first = jnp.int32(-1)
     second = jnp.int32(0)
@@ -607,9 +607,21 @@
         first = jnp.where(moves & (first < 0), i, first)
     first = jnp.maximum(first, 0)
     rows = iota((16, 1024), 0) & 3
+    states = [mid[first], mid[second]]
+    late_swap.wait_recv()
+    late_sum = late_sum + late_half_land[...].astype(F32)
+    main = late_sum[:, 0:128]
+    square = jnp.broadcast_to(jnp.sum(main * main, axis=1, keepdims=True), (16, 128))
+    square = square + pltpu.roll(square, 8, 0)
+    square = square + pltpu.roll(square, 4, 0)
+    low = (main * lax.rsqrt(square / 512.0 + EPS) * gains).astype(BF16)
+    spread = nn(widen, low)
+    low = jnp.concatenate([spread[b * 16 : (b + 1) * 16] for b in range(4)], axis=1)
+    late_dt = softplus(nn(low.astype(BF16), dw[...]) + dtb_ref[...])
+    late_tail = tail_norm(late_sum[:, 128:256])
+
     late_mixed = jnp.zeros((16, 1024), F32)
-    for r, slot in enumerate((first, second)):
-        state = mid[slot]
+    for r, state in enumerate(states):
         for s in range(2):
             m = r * 2 + s
             state, out = advance(
@@ -619,22 +631,24 @@
     gather_m[0] = by_quarter(
         [late_mixed[:, b * 256 : (b + 1) * 256] for b in range(4)]
     ).astype(BF16)
-    z_m = [push(gather_m.at[0], gather_m.at[d], (z_rep(d), tp)) for d in range(1, nz)]
+    z_m = send_all(gather_m.at[0], gather_m, columns_z)
 
     scan(2, mid, False)
     need("z_ref")
     partial.wait_recv()
     kept = []
+    gates = []
     for s in range(4):
+        gate = silu(z_ref[s].astype(F32))
         block = combine(near[s * 64 : (s + 1) * 64, :], far[s * 64 : (s + 1) * 64, :])
         block = jnp.concatenate([block[h * 16 : (h + 1) * 16] for h in range(4)], axis=1)
         if s < 2:
             attn_ref[s] = block.astype(BF16)
-            mix_ref[s] = (mixed[s] * silu(z_ref[s].astype(F32))).astype(BF16)
+            mix_ref[s] = (mixed[s] * gate).astype(BF16)
         else:
             kept.append(block)
-
-    y_a = select(z_a, select_out, gather_a, stage_a, land_a)
+            gates.append((gate, mixed[s] * gate))
+
     own_code = rep * 2 + ((iota((ny * 16, n), 0) >> 1) & 1)
     fr = iota((128, ny * 16), 0)
     fc = iota((128, ny * 16), 1)
@@ -644,17 +658,21 @@
         & (nt(slot_pick, hot(home == own_code)) > 0.5)
     )
     y_m = select(z_m, select_out, gather_m, stage_m, land_m)
-    for copy in y_a + y_m:
+    y_a = select(z_a, select_out, gather_a, stage_a, land_a)
+    spots = [[s * 64 + b * 16 for b in range(4)] for s in range(2)]
+    for copy in y_a:
+        copy.wait_recv()
+    attended = nn(put, land_a[...].reshape(ny * 16, 128))
+    for s in range(2):
+        back = jnp.concatenate([attended[p : p + 16] for p in spots[s]], axis=1)
+        attn_ref[s + 2] = jnp.where(foreign_col, back, kept[s]).astype(BF16)
+    for copy in y_m:
         copy.wait_recv()
     returned = nn(put, land_m[...].reshape(ny * 16, 256))
-    attended = nn(put, land_a[...].reshape(ny * 16, 128))
-    for s in (2, 3):
-        spots = [(s - 2) * 64 + b * 16 for b in range(4)]
-        back = jnp.concatenate([returned[p : p + 16] for p in spots], axis=1)
-        whole = jnp.where(foreign_col, back, mixed[s])
-        mix_ref[s] = (whole * silu(z_ref[s].astype(F32))).astype(BF16)
-        back = jnp.concatenate([attended[p : p + 16] for p in spots], axis=1)
-        attn_ref[s] = jnp.where(foreign_col, back, kept[s - 2]).astype(BF16)
+    for s in range(2):
+        back = jnp.concatenate([returned[p : p + 16] for p in spots[s]], axis=1)
+        gate, own_mix = gates[s]
+        mix_ref[s + 2] = jnp.where(foreign_col, back * gate, own_mix).astype(BF16)
 
     for copy in used:
         copy.wait_send()

time: 51.2 us -> 51.2 us (level)
  no operation moved by 1% of the time
where the time goes in v6:
time: 51.2 us; the launch traced here: 51 us
  Pallas kernels  49.1 us (96%)
  local copies, waits for them, and re-layouts  1.29 us (3%)
  between operations  0.65 us (1%)
    pallas_call x1, Pallas kernels, shards(): pl.pallas_call(functools.partial(kernel, geo), out_shape=(pltpu.VMEM(quer...  49.1 us
    unnamed x2, local copies, waits for them, and re-layouts  1.29 us

profile of v6, /device:TPU:1, one launch (start us, length us, event | category | flops | bytes accessed | tf_op | source)
XLA Modules:
  0.0 51.0 jit_solution(1685022891180714996)
XLA Ops:
  0.6 49.1 %shard_map.203 = (bf16[4,16,512]{2,1,0:T(8,128)(2,1)S(1)}, bf16[4,16,1024]{2,1,0:T(8,128)(2,1)S(1)}) custom-call(s32[1,512]{1,0:T(1,128)} %bitcast.11, bf16[4,16,512]{2,1,0:T(8,128)(2,1)} %q_ref_h.1, bf16[4,16,128]{2,1,0:T(8,128)(2,1)} %nk_ref_h.1, bf16[4,16,1024]{2,1,0:T(8,128)(2,1)} %x_ref_h.1, s32[512]{0:T(512)} %src_s_h.1, ...), custom_call_target="tpu_custom_call" | custom-call | tf_op jit(solution)/shard_map/pallas_call | solution.py:779
  49.8 0.6 %copy.24 = bf16[4,16,512]{2,1,0:T(8,128)(2,1)} copy(bf16[4,16,512]{2,1,0:T(8,128)(2,1)S(1)} %get-tuple-element.2) | data formatting | bytes 131072
  50.4 0.7 %copy.25 = bf16[4,16,1024]{2,1,0:T(8,128)(2,1)} copy(bf16[4,16,1024]{2,1,0:T(8,128)(2,1)S(1)} %get-tuple-element.3) | data formatting | bytes 262144

commit v7 on v6

--- a/solution.py
+++ b/solution.py
@@ -621,11 +621,11 @@
     late_tail = tail_norm(late_sum[:, 128:256])
 
     late_mixed = jnp.zeros((16, 1024), F32)
-    for r, state in enumerate(states):
-        for s in range(2):
+    for s in range(2):
+        for r in range(2):
             m = r * 2 + s
-            state, out = advance(
-                state, late_dt[m : m + 1], late_act[m : m + 1], late_tail[m : m + 1]
+            states[r], out = advance(
+                states[r], late_dt[m : m + 1], late_act[m : m + 1], late_tail[m : m + 1]
             )
             late_mixed = jnp.where(rows == m, out, late_mixed)
     gather_m[0] = by_quarter(

time: 51.2 us -> 51.2 us (level)
  no operation moved by 1% of the time
where the time goes in v7:
time: 51.2 us; the launch traced here: 51 us
  Pallas kernels  49.1 us (96%)
  local copies, waits for them, and re-layouts  1.29 us (3%)
  between operations  0.65 us (1%)
    pallas_call x1, Pallas kernels, shards(): pl.pallas_call(functools.partial(kernel, geo), out_shape=(pltpu.VMEM(quer...  49.1 us
    unnamed x2, local copies, waits for them, and re-layouts  1.29 us

profile of v7, /device:TPU:1, one launch (start us, length us, event | category | flops | bytes accessed | tf_op | source)
XLA Modules:
  0.0 51.0 jit_solution(3515852004557736238)
XLA Ops:
  0.6 49.1 %shard_map.203 = (bf16[4,16,512]{2,1,0:T(8,128)(2,1)S(1)}, bf16[4,16,1024]{2,1,0:T(8,128)(2,1)S(1)}) custom-call(s32[1,512]{1,0:T(1,128)} %bitcast.11, bf16[4,16,512]{2,1,0:T(8,128)(2,1)} %q_ref_h.1, bf16[4,16,128]{2,1,0:T(8,128)(2,1)} %nk_ref_h.1, bf16[4,16,1024]{2,1,0:T(8,128)(2,1)} %x_ref_h.1, s32[512]{0:T(512)} %src_s_h.1, ...), custom_call_target="tpu_custom_call" | custom-call | tf_op jit(solution)/shard_map/pallas_call | solution.py:779
  49.8 0.6 %copy.24 = bf16[4,16,512]{2,1,0:T(8,128)(2,1)} copy(bf16[4,16,512]{2,1,0:T(8,128)(2,1)S(1)} %get-tuple-element.2) | data formatting | bytes 131072
  50.4 0.7 %copy.25 = bf16[4,16,1024]{2,1,0:T(8,128)(2,1)} copy(bf16[4,16,1024]{2,1,0:T(8,128)(2,1)S(1)} %get-tuple-element.3) | data formatting | bytes 262144
